TPU v7x, 256 devices: a whole 4x4x8 slice. The times are simulated.
256 devices in a mesh: row: 8 (over y, core), col: 32 (over z, x).
Axes of the slice: x: 4, y: 4, z: 8, core: 2. Of those that a mesh axis runs over, the one named last changes fastest.
Arguments:
- prior_factors: float32 [16384, 128], P(('row', 'col')), may hold values from -6 to 6
- item_factors: bfloat16 [262144, 128], P(('row', 'col')), may hold values from -1 to 1
- user_tiles: int32 [8, 32, 40], P('row', 'col'), may hold values from 0 to 7
- item_tiles: int32 [8, 32, 40], P('row', 'col'), may hold values from 0 to 31
- tile_counts: int32 [8, 32], P('row', 'col'), may hold values from 10 to 40, as said below
- ratings: int32 [8, 32, 40, 256, 256], P('row', 'col'), may hold values from 0 to 5
Outputs:
- new_factors: float32 [16384, 128], P(('row', 'col'))
- residual: float32 [16384, 128], P(('row', 'col'))
Inputs may be any that keep to these rules, and one draw needn't show every extreme that they name: `tile_counts`: some block has all 40 slots live in every draw.
All inputs are finite; a program needn't handle non-finite values.
Results may differ from a plain program's by a relative error of at most 0.012.
The roundings to bfloat16 on the way count: a program that leaves them out, or rounds other values in their place, can miss the bound.
Values may be sent and summed in bfloat16 or wider, within the bound.
No kernel may reach another device: no remote copies, remote signals or barrier semaphores. Data moves between devices by JAX's collectives and lax.ppermute only.
A program may use at most 128 MiB of HBM per device.

v0:
```python
import jax
import jax.numpy as jnp
from jax import lax
from jax.sharding import PartitionSpec as P

RANK = 128
TILE = 256
ITERS = 3


confidence = 40.0
ridge_term = 0.1


def tile_term(rows, item_panel, users, items, count, rates, first):
    slot_count = users.shape[0]
    user_blocks = rows.reshape(-1, TILE, RANK)[users]
    item_blocks = item_panel.reshape(-1, TILE, RANK)[items]
    scores = jnp.einsum(
        "tuk,tik->tui", user_blocks, item_blocks, preferred_element_type=jnp.float32
    )
    rate = rates.astype(jnp.float32)
    live = (jnp.arange(slot_count) < count)[:, None, None]
    if first:
        coef = jnp.where(rate > 0, 1.0 + confidence * rate * (1.0 - scores), 0.0)
    else:
        coef = confidence * rate * scores
    coef = jnp.where(live, coef, 0.0).astype(jnp.bfloat16)
    contrib = jnp.einsum("tui,tik->tuk", coef, item_blocks, preferred_element_type=jnp.float32)
    blocks = rows.shape[0] // TILE
    onehot = (users[None, :] == jnp.arange(blocks)[:, None]).astype(jnp.float32)
    summed = jnp.dot(
        onehot, contrib.reshape(slot_count, TILE * RANK), precision=lax.Precision.HIGHEST
    )
    return summed.reshape(rows.shape[0], RANK)


def body(prior_factors, item_factors, user_tiles, item_tiles, tile_counts, ratings):
    users = user_tiles[0, 0]
    items = item_tiles[0, 0]
    count = tile_counts[0, 0]
    rates = ratings[0, 0]
    item_panel = lax.all_gather(item_factors, "row", axis=0, tiled=True)
    local_gram = lax.dot_general(
        item_factors, item_factors, (((0,), (0,)), ((), ())), preferred_element_type=jnp.float32
    )
    gram_matrix = lax.psum(local_gram, ("row", "col"))
    shifted = gram_matrix + ridge_term * jnp.eye(RANK, dtype=jnp.float32)

    def apply_shift(field):
        return jnp.dot(field, shifted, precision=lax.Precision.HIGHEST)

    def group_term(rows, first):
        return tile_term(rows, item_panel, users, items, count, rates, first)

    start_group = lax.all_gather(prior_factors.astype(jnp.bfloat16), "col", axis=0, tiled=True)
    start_part = lax.psum_scatter(
        group_term(start_group, True), "col", scatter_dimension=0, tiled=True
    )
    new_factors = prior_factors
    residual = start_part - apply_shift(prior_factors)
    direction = residual
    norm_now = jnp.sum(residual * residual, axis=1, keepdims=True)
    for iteration in range(ITERS):
        gathered = lax.all_gather(direction.astype(jnp.bfloat16), "col", axis=0, tiled=True)
        image = lax.psum_scatter(
            group_term(gathered, False), "col", scatter_dimension=0, tiled=True
        ) + apply_shift(direction)
        step_size = norm_now / jnp.sum(direction * image, axis=1, keepdims=True)
        new_factors = new_factors + step_size * direction
        residual = residual - step_size * image
        norm_next = jnp.sum(residual * residual, axis=1, keepdims=True)
        direction = residual + norm_next / norm_now * direction
        norm_now = norm_next
    return (new_factors, residual)


def solution(mesh):
    placed = (
        P(("row", "col"), None),
        P(("row", "col"), None),
        P("row", "col", None),
        P("row", "col", None),
        P("row", "col"),
        P("row", "col", None, None, None),
    )
    return jax.shard_map(
        body,
        mesh=mesh,
        in_specs=placed,
        out_specs=(P(("row", "col"), None), P(("row", "col"), None)),
        check_vma=False,
    )
```

profile of v0, /device:TPU:1, one launch (start us, length us, event | category | flops | bytes accessed | tf_op | source)
XLA Modules:
  0.0 1159.8 jit_solution(8659801345296993141)
XLA Ops:
  8.0 0.0 all-gather.2.cloned.1.call-start
  8.0 0.7 all-gather.2.cloned.1.call-update
  8.7 0.0 all-reduce.2.cloned.1.call-start
  8.8 1.9 fusion.76
  10.7 0.0 all-reduce.2.cloned.1.call-update
  10.7 0.0 reduce-scatter.5.cloned.1.call-start
  11.4 0.7 fusion.55
  12.1 0.7 fusion.54
  12.8 0.8 convert_element_type.37
  13.5 45.0 %all_gather.15 = bf16[2048,128]{1,0:T(8,128)(2,1)S(1)} all-gather(bf16[64,128]{1,0:T(8,128)(2,1)S(1)} %convert_element_type.37), channel_id=1, replica_groups=mesh['row'=8,'col'=32] {'col'}, dimensions={0}, use_global_device_ids=true | all-gather | bytes 540672 | tf_op jit(solution)/shard_map/all_gather | solution.py:56
  58.6 2.5 gather_fusion
  61.1 2.6 gather_fusion.1
  63.8 8.3 fusion.35
  72.1 8.0 fusion.26
  80.1 2.4 reshape.145
  82.5 0.0 reduce-scatter.5.cloned.1.call-update
  82.5 0.0 reduce-scatter.7.cloned.1.call-start
  82.6 176.1 %all-reduce.2.cloned.1.call-done = f32[128,128]{1,0:T(8,128)} async-done(((f32[128,128]{1,0:T(8,128)}), f32[128,128]{1,0:T(8,128)}) %all-reduce.2.cloned.1.call-update) | async-done | bytes 65552 | tf_op jit(solution)/shard_map/psum | solution.py:47
  258.7 38.9 %reduce-scatter.5.cloned.1.call-done = f32[64,128]{1,0:T(8,128)} async-done(((f32[2048,128]{1,0:T(8,128)}), f32[64,128]{1,0:T(8,128)}) %reduce-scatter.5.cloned.1.call-update) | async-done | bytes 32784 | tf_op jit(solution)/shard_map/reduce_scatter | solution.py:57
  297.6 1.0 fusion.75
  298.7 36.7 %all_gather.17 = bf16[2048,128]{1,0:T(8,128)(2,1)S(1)} all-gather(bf16[64,128]{1,0:T(8,128)(2,1)S(1)} %get-tuple-element.12), channel_id=1, replica_groups=mesh['row'=8,'col'=32] {'col'}, dimensions={0}, use_global_device_ids=true | all-gather | bytes 540672 | tf_op jit(solution)/shard_map/all_gather | solution.py:65
  335.4 2.5 gather_fusion.2
  337.9 10.0 fusion.15
  347.9 8.1 fusion.23
  356.0 2.4 reshape.148
  358.4 0.0 reduce-scatter.9.cloned.1.call-start
  358.4 223.8 %reduce-scatter.7.cloned.1.call-done = f32[64,128]{1,0:T(8,128)} async-done(((f32[2048,128]{1,0:T(8,128)}), f32[64,128]{1,0:T(8,128)}) %reduce-scatter.7.cloned.1.call-update) | async-done | bytes 32784 | tf_op jit(solution)/shard_map/reduce_scatter | solution.py:66
  582.2 1.0 multiply_reduce_fusion.4
  583.3 0.2 multiply_reduce_fusion.3
  583.5 0.1 fusion.74
  583.6 36.0 %all_gather.18 = bf16[2048,128]{1,0:T(8,128)(2,1)S(1)} all-gather(bf16[64,128]{1,0:T(8,128)(2,1)S(1)} %get-tuple-element.8), channel_id=1, replica_groups=mesh['row'=8,'col'=32] {'col'}, dimensions={0}, use_global_device_ids=true | all-gather | bytes 540672 | tf_op jit(solution)/shard_map/all_gather | solution.py:65
  619.7 2.5 gather_fusion.3
  622.2 10.0 fusion.13
  632.2 8.0 fusion.20
  640.2 2.4 reshape.151
  642.6 0.0 reduce-scatter.11.cloned.1.call-start
  642.7 224.6 %reduce-scatter.9.cloned.1.call-done = f32[64,128]{1,0:T(8,128)} async-done(((f32[2048,128]{1,0:T(8,128)}), f32[64,128]{1,0:T(8,128)}) %reduce-scatter.9.cloned.1.call-update) | async-done | bytes 32784 | tf_op jit(solution)/shard_map/reduce_scatter | solution.py:66
  867.3 1.0 multiply_reduce_fusion.2
  868.4 0.2 multiply_reduce_fusion.1
  868.6 0.1 fusion.73
  868.7 36.0 %all_gather.19 = bf16[2048,128]{1,0:T(8,128)(2,1)S(1)} all-gather(bf16[64,128]{1,0:T(8,128)(2,1)S(1)} %get-tuple-element.4), channel_id=1, replica_groups=mesh['row'=8,'col'=32] {'col'}, dimensions={0}, use_global_device_ids=true | all-gather | bytes 540672 | tf_op jit(solution)/shard_map/all_gather | solution.py:65
  904.7 2.5 gather_fusion.4
  907.2 10.0 fusion.11
  917.2 7.0 fusion.17
  924.2 1.1 reshape.154
  925.4 225.0 %reduce-scatter.11.cloned.1.call-done = f32[64,128]{1,0:T(8,128)} async-done(((f32[2048,128]{1,0:T(8,128)}), f32[64,128]{1,0:T(8,128)}) %reduce-scatter.11.cloned.1.call-update) | async-done | bytes 32784 | tf_op jit(solution)/shard_map/reduce_scatter | solution.py:66
  1150.4 1.0 multiply_reduce_fusion
  1151.5 0.7 multiply_subtract_fusion
  (18 shorter events, 0.1 us)
Async XLA Ops:
  8.0 53.1 %all-gather.2.cloned.1.call-start = ((), (), s32[]{:S(2)}) async-start(), calls=%async_computation.4 | async-start | bytes 2359296 | tf_op jit(solution)/shard_map/all_gather | solution.py:43
  8.7 250.0 %all-reduce.2.cloned.1.call-start = ((), (), s32[]{:S(2)}) async-start(), calls=%async_computation.6 | async-start | bytes 131072 | tf_op jit(solution)/shard_map/psum | solution.py:47
  10.7 286.9 %reduce-scatter.5.cloned.1.call-start = ((), (), s32[]{:S(2)}) async-start(), calls=%async_computation.5 | async-start | bytes 1081344 | tf_op jit(solution)/shard_map/reduce_scatter | solution.py:57
  63.8 8.3 copy-start.2
  72.1 225.5 %copy-start.1 = (f32[64,128]{1,0:T(8,128)S(1)}, f32[64,128]{1,0:T(8,128)}, u32[]{:S(2)}) copy-start(f32[64,128]{1,0:T(8,128)} %param.6) | copy-start | bytes 98308
  82.5 499.7 %reduce-scatter.7.cloned.1.call-start = ((), (), s32[]{:S(2)}) async-start(), calls=%async_computation.7 | async-start | bytes 1081344 | tf_op jit(solution)/shard_map/reduce_scatter | solution.py:66
  347.9 234.3 %copy-start = (f32[128,128]{1,0:T(8,128)S(1)}, f32[128,128]{1,0:T(8,128)}, u32[]{:S(2)}) copy-start(f32[128,128]{1,0:T(8,128)} %all-reduce.2.cloned.1.call-done) | copy-start | bytes 196612
  358.4 509.0 %reduce-scatter.9.cloned.1.call-start = ((), (), s32[]{:S(2)}) async-start(), calls=%async_computation.8 | async-start | bytes 1081344 | tf_op jit(solution)/shard_map/reduce_scatter | solution.py:66
  642.6 507.8 %reduce-scatter.11.cloned.1.call-start = ((), (), s32[]{:S(2)}) async-start(), calls=%async_computation.9 | async-start | bytes 1081344 | tf_op jit(solution)/shard_map/reduce_scatter | solution.py:66
Sparse Core Ops, SparseCore 0:
  10.7 31.9 all-gather.1
  82.7 214.9 reduce-scatter.4
  358.5 223.7 reduce-scatter.6
  642.8 224.5 reduce-scatter.8
  925.5 224.8 reduce-scatter.10
Sparse Core Ops, SparseCore 1:
  14.7 243.9 all-reduce.1
where the time goes:
time: 1170 us; the launch traced here: 1160 us
  waiting for transfers between devices  889 us (76%)
  blocking collectives  154 us (13%)
  matrix products  75.5 us (6%)
  local copies, waits for them, and re-layouts  21.1 us (2%)
  between operations  16.4 us (1%)
    reduce_scatter x3, waiting for transfers between devices, body(): lax.psum_scatter(group_term(gathered, False), 'col', scatter_dimension=0,...  674 us
    psum x1, waiting for transfers between devices, body(): gram_matrix = lax.psum(local_gram, ('row', 'col'))  176 us
    all_gather x3, blocking collectives, body(): lax.all_gather(direction.astype(jnp.bfloat16), 'col', axis=0, tiled=True)  109 us
    all_gather x1, blocking collectives, body(): lax.all_gather(prior_factors.astype(jnp.bfloat16), 'col', axis=0, tiled=T...  45 us
    reduce_scatter x1, waiting for transfers between devices, body(): lax.psum_scatter(group_term(start_group, True), 'col', scatter_dimension=...  38.9 us
    dot_general x4, matrix products, tile_term(): jnp.einsum('tui,tik->tuk', coef, item_blocks, preferred_element_type=jnp....  38.3 us
    dot_general x4, matrix products, tile_term(): jnp.dot(onehot, contrib.reshape(slot_count, TILE * RANK), precision=lax.P...  31.1 us
  transfers between devices with their start and end apart: 6, of which 5 were waited for; matrix products, arithmetic and copies ran while one was open for 2% of the time, Pallas kernels for 0%

commit v1 on v0

v1 whole, which is shorter than its diff:
```python
import functools

import jax
import jax.numpy as jnp
from jax import lax
from jax.experimental import pallas as pl
from jax.experimental.pallas import tpu as pltpu
from jax.sharding import PartitionSpec as P

RANK = 128
TILE = 256
ITERS = 3
GRAM_PAD = 8
GRAM_PARTS = 16

confidence = 40.0
ridge_term = 0.1

bf16 = jnp.bfloat16
f32 = jnp.float32
VMEM_LIMIT = 56 * 1024 * 1024


def params():
    return pltpu.CompilerParams(vmem_limit_bytes=VMEM_LIMIT)


def rate_kernel(step_slots, count_ref, rates_ref, out_ref):
    base = pl.program_id(0) * step_slots
    for j in range(step_slots):
        weight = jnp.where(base + j < count_ref[0], confidence, 0.0)
        out_ref[j] = (rates_ref[j].astype(f32) * weight).astype(bf16)


def scale_rates(count, rates):
    slots = rates.shape[0]
    step_slots = 4
    return pl.pallas_call(
        functools.partial(rate_kernel, step_slots),
        grid_spec=pltpu.PrefetchScalarGridSpec(
            num_scalar_prefetch=1,
            grid=(slots // step_slots,),
            in_specs=[pl.BlockSpec((step_slots, TILE, TILE), lambda i, c: (i, 0, 0))],
            out_specs=pl.BlockSpec((step_slots, TILE, TILE), lambda i, c: (i, 0, 0)),
        ),
        out_shape=jax.ShapeDtypeStruct(rates.shape, bf16),
        compiler_params=params(),
        name="scale_rates",
    )(count, rates)


def split2(x):
    high = x.astype(bf16)
    return high, (x - high.astype(f32)).astype(bf16)


def tile_kernel(first, n_peer, own, users_ref, items_ref, rates_hbm, rows_ref, panel_ref, *rest):
    if first:
        gram_ref, out_ref, rates, sems = rest
    else:
        out_ref, rates, sems = rest
    chunks = sems.shape[0]
    per = rates.shape[0] // chunks
    peers = TILE // own

    def copy(k):
        part = pl.ds(k * per, per)
        return pltpu.make_async_copy(rates_hbm.at[part], rates.at[part], sems.at[k])

    for k in range(chunks):
        copy(k).start()
    if first:
        gram = gram_ref[...]
        gram_high, gram_low = split2(gram)
        for p in range(n_peer):
            high = rows_ref[p, :own]
            low = rows_ref[p, own:2 * own]
            shift = jnp.dot(high, gram_high, preferred_element_type=f32)
            shift += jnp.dot(high, gram_low, preferred_element_type=f32)
            shift += jnp.dot(low, gram_high, preferred_element_type=f32)
            out_ref[p, :own] = -shift
            out_ref[p, own:own + 4] = gram[4 * p:4 * p + 4]
            out_ref[p, own + 4:] = jnp.zeros((GRAM_PAD - 4, RANK), f32)
    else:
        out_ref[...] = jnp.zeros_like(out_ref)

    def slot(s):
        user = users_ref[s] * peers
        item = pl.multiple_of(items_ref[s] * TILE, TILE)
        block = panel_ref[pl.ds(item, TILE), :]
        field = rows_ref[pl.ds(user, peers), :own].reshape(TILE, RANK)
        scores = lax.dot_general(
            field, block, (((1,), (1,)), ((), ())), preferred_element_type=f32
        )
        rate = rates[s].astype(f32)
        if first:
            coef = jnp.where(rate > 0, 1.0 + rate * (1.0 - scores), 0.0)
        else:
            coef = rate * scores
        contrib = jnp.dot(coef.astype(bf16), block, preferred_element_type=f32)
        out_ref[pl.ds(user, peers), :own] += contrib.reshape(peers, own, RANK)

    for k in range(chunks):
        copy(k).wait()

        def pair(i, carry):
            slot(k * per + 2 * i)
            slot(k * per + 2 * i + 1)
            return carry

        lax.fori_loop(0, per // 2, pair, 0)


def tile_pass(first, users, items, rates, rows, panel, own, gram=None):
    n_peer = rows.shape[0]
    slots = rates.shape[0]
    chunks = 5
    vmem = pl.BlockSpec(memory_space=pltpu.VMEM)
    smem = pl.BlockSpec(memory_space=pltpu.SMEM)
    out_rows = own + (GRAM_PAD if first else 0)
    operands = (users, items, rates, rows, panel) + ((gram,) if first else ())
    return pl.pallas_call(
        functools.partial(tile_kernel, first, n_peer, own),
        in_specs=[smem, smem, pl.BlockSpec(memory_space=pl.ANY)] + [vmem] * (len(operands) - 3),
        out_specs=vmem,
        out_shape=jax.ShapeDtypeStruct((n_peer, out_rows, RANK), f32),
        scratch_shapes=[
            pltpu.VMEM((slots, TILE, TILE), bf16),
            pltpu.SemaphoreType.DMA((chunks,)),
        ],
        compiler_params=params(),
        name="tile_start" if first else "tile_pass",
    )(*operands)


def start_update_kernel(own, parts_ref, prior_ref, residual_ref, sent_ref):
    total = jnp.sum(parts_ref[...], axis=0)
    residual = total[:own] - ridge_term * prior_ref[...]
    residual_ref[...] = residual
    gram = total[own:]
    gram_high, rest = split2(gram)
    rest = gram - gram_high.astype(f32)
    gram_mid, gram_low = split2(rest)
    pack = jnp.concatenate(
        [gram_high.astype(f32)[:4], gram_mid.astype(f32)[:4], gram_low.astype(f32)[:4],
         jnp.zeros((4, RANK), f32)], axis=0
    ).astype(bf16)
    sent = jnp.concatenate([residual.astype(bf16), pack], axis=0)
    sent_ref[...] = jnp.broadcast_to(sent[None], sent_ref.shape)


def start_update(parts, prior):
    n_peer = parts.shape[0]
    own = prior.shape[0]
    vmem = pl.BlockSpec(memory_space=pltpu.VMEM)
    return pl.pallas_call(
        functools.partial(start_update_kernel, own),
        in_specs=[vmem] * 2,
        out_specs=[vmem] * 2,
        out_shape=[
            jax.ShapeDtypeStruct(prior.shape, f32),
            jax.ShapeDtypeStruct((n_peer, own + GRAM_PARTS, RANK), bf16),
        ],
        compiler_params=params(),
        name="start_update",
    )(parts, prior)


def update_kernel(last, parts_ref, shift_ref, factors_ref, residual_ref, direction_ref, *outs):
    direction = direction_ref[...]
    residual = residual_ref[...]
    shift = jnp.dot(
        direction, shift_ref[...], precision=lax.Precision.HIGHEST, preferred_element_type=f32
    )
    image = jnp.sum(parts_ref[...].astype(f32), axis=0) + shift
    norm_now = jnp.sum(residual * residual, axis=1, keepdims=True)
    step_size = norm_now / jnp.sum(direction * image, axis=1, keepdims=True)
    outs[0][...] = factors_ref[...] + step_size * direction
    residual = residual - step_size * image
    outs[1][...] = residual
    if not last:
        norm_next = jnp.sum(residual * residual, axis=1, keepdims=True)
        direction = residual + norm_next / norm_now * direction
        outs[2][...] = direction
        outs[3][...] = jnp.broadcast_to(direction.astype(bf16)[None], outs[3].shape)


def update(last, parts, shifted, factors, residual, direction):
    n_peer = parts.shape[0]
    own = factors.shape[0]
    vmem = pl.BlockSpec(memory_space=pltpu.VMEM)
    state = jax.ShapeDtypeStruct(factors.shape, f32)
    shapes = [state] * 2
    if not last:
        shapes += [state, jax.ShapeDtypeStruct((n_peer, own, RANK), bf16)]
    return pl.pallas_call(
        functools.partial(update_kernel, last),
        in_specs=[vmem] * 5,
        out_specs=[vmem] * len(shapes),
        out_shape=shapes,
        compiler_params=params(),
        name="update_last" if last else "update",
    )(parts, shifted, factors, residual, direction)


def exchange(blocks):
    return lax.all_to_all(blocks, "col", 0, 0, tiled=True)


def body(prior_factors, item_factors, user_tiles, item_tiles, tile_counts, ratings):
    users = user_tiles[0, 0]
    items = item_tiles[0, 0]
    own = prior_factors.shape[0]
    n_peer = lax.axis_size("col")
    panel = lax.all_gather(item_factors, "row", axis=0, tiled=True)
    rates = scale_rates(tile_counts[0], ratings[0, 0])
    high = lax.reduce_precision(prior_factors, 8, 7)
    rows = jnp.concatenate([high, prior_factors - high], axis=0).astype(bf16)
    rows = exchange(jnp.broadcast_to(rows[None], (n_peer,) + rows.shape))
    gram = lax.dot_general(
        panel, panel, (((0,), (0,)), ((), ())), preferred_element_type=f32
    )
    parts = exchange(tile_pass(True, users, items, rates, rows, panel, own, gram))
    residual, sent = start_update(parts, prior_factors)
    direction = residual
    factors = prior_factors
    rows = exchange(sent)
    parts = rows[:, own:].astype(f32)
    gram = (parts[:, :4] + parts[:, 4:8] + parts[:, 8:12]).reshape(RANK, RANK)
    shifted = gram + ridge_term * jnp.eye(RANK, dtype=f32)
    for iteration in range(ITERS):
        last = iteration == ITERS - 1
        parts = tile_pass(False, users, items, rates, rows, panel, own)
        parts = exchange(parts)
        out = update(last, parts, shifted, factors, residual, direction)
        if last:
            return tuple(out)
        factors, residual, direction, sent = out
        rows = exchange(sent)


def solution(mesh):
    placed = (
        P(("row", "col"), None),
        P(("row", "col"), None),
        P("row", "col", None),
        P("row", "col", None),
        P("row", "col"),
        P("row", "col", None, None, None),
    )
    return jax.shard_map(
        body,
        mesh=mesh,
        in_specs=placed,
        out_specs=(P(("row", "col"), None), P(("row", "col"), None)),
        check_vma=False,
    )
```

time: 1170 us -> 320 us (0.27)
  the two profiles are of different devices: /device:TPU:1 before, /device:TPU:2 now
where the time goes in v1:
time: 320 us; the launch traced here: 319 us
  blocking collectives  160 us (50%)
  Pallas kernels  77.9 us (24%)
  waiting for transfers between devices  39.4 us (12%)
  starting transfers between devices  17.2 us (5%)
  between operations  14.7 us (5%)
  matrix products  3.6 us (1%)
  local copies, waits for them, and re-layouts  3.34 us (1%)
    all_to_all x6, blocking collectives, exchange(): return lax.all_to_all(blocks, 'col', 0, 0, tiled=True)  160 us
    pallas_call x4, Pallas kernels, tile_pass(): pl.pallas_call(functools.partial(tile_kernel, first, n_peer, own), in_spe...  58.9 us
    all_to_all x2, waiting for transfers between devices, exchange(): return lax.all_to_all(blocks, 'col', 0, 0, tiled=True)  29.9 us
    all_to_all x2, starting transfers between devices, exchange(): return lax.all_to_all(blocks, 'col', 0, 0, tiled=True)  17.2 us
    pallas_call x1, Pallas kernels, scale_rates(): pl.pallas_call(functools.partial(rate_kernel, step_slots), grid_spec=pltp...  9.54 us
    all_gather x1, waiting for transfers between devices, body(): panel = lax.all_gather(item_factors, 'row', axis=0, tiled=True)  8.84 us
    pallas_call x3, Pallas kernels, update(): pl.pallas_call(functools.partial(update_kernel, last), in_specs=[vmem] *...  7.22 us
  transfers between devices with their start and end apart: 3, of which 3 were waited for; matrix products, arithmetic and copies ran while one was open for 2% of the time, Pallas kernels for 3%

profile of v1, /device:TPU:2, one launch (start us, length us, event | category | flops | bytes accessed | tf_op | source)
XLA Modules:
  0.0 318.6 jit_solution(3835808361306528367)
XLA Ops:
  7.2 0.0 all-gather.2.cloned.1.call-start
  7.2 0.7 all-gather.2.cloned.1.call-update
  7.9 0.8 reduce-precision_convert_fusion
  8.7 1.2 broadcast_in_dim.2
  9.9 11.6 %all-to-all-start = ((bf16[32,128,128]{2,1,0:T(8,128)(2,1)}), bf16[32,128,128]{2,1,0:T(8,128)(2,1)S(1)}, u32[]{:S(2)}, u32[]{:S(2)}) async-start(bf16[32,128,128]{2,1,0:T(8,128)(2,1)} %broadcast_in_dim.2), calls=%async_computation | async-start | bytes 2097152 | tf_op jit(solution)/shard_map/all_to_all | solution.py:207
  22.2 9.5 %scale_rates.1.rates_hbm = bf16[40,256,256]{2,1,0:T(8,128)(2,1)} custom-call(s32[1]{0:T(128)} %bitcast.7.count_ref, s32[40,256,256]{2,1,0:T(8,128)} %bitcast.8), custom_call_target="tpu_custom_call" | custom-call | tf_op jit(solution)/shard_map/scale_rates/pallas_call | solution.py:38
  31.7 8.8 %all-gather.2.cloned.1.call-done.panel_ref = bf16[8192,128]{1,0:T(8,128)(2,1)} async-done(((bf16[1024,128]{1,0:T(8,128)(2,1)}), bf16[8192,128]{1,0:T(8,128)(2,1)}) %all-gather.2.cloned.1.call-update) | async-done | bytes 2097168 | tf_op jit(solution)/shard_map/all_gather | solution.py:215
  40.6 3.6 %fusion.1.rest_0_ = f32[128,128]{1,0:T(8,128)} fusion(bf16[8192,128]{1,0:T(8,128)(2,1)} %all-gather.2.cloned.1.call-done.panel_ref), kind=kOutput, calls=%fused_computation.9 | convolution fusion | flops 268435456 | bytes 2162688 | tf_op jit(solution)/shard_map/dot_general | solution.py:220
  44.2 5.4 %all-to-all-done.rows_ref = bf16[32,128,128]{2,1,0:T(8,128)(2,1)S(1)} async-done(((bf16[32,128,128]{2,1,0:T(8,128)(2,1)}), bf16[32,128,128]{2,1,0:T(8,128)(2,1)S(1)}, u32[]{:S(2)}, u32[]{:S(2)}) %all-to-all-start) | async-done | bytes 1048608 | tf_op jit(solution)/shard_map/all_to_all | solution.py:207
  49.6 0.0 copy-start
  49.6 1.1 copy-done
  50.7 14.9 %tile_start.1 = f32[32,72,128]{2,1,0:T(8,128)} custom-call(s32[40]{0:T(128)} %bitcast.10, s32[40]{0:T(128)} %bitcast.14, bf16[40,256,256]{2,1,0:T(8,128)(2,1)} %scale_rates.1.rates_hbm, bf16[32,128,128]{2,1,0:T(8,128)(2,1)} %copy-done, bf16[8192,128]{1,0:T(8,128)(2,1)} %all-gather.2.cloned.1.call-done.panel_ref, f32[128,128]{1,0:T(8,128)} %fusion.1.rest_0_), custom_call_target="tpu_custom_call" | custom-call | tf_op jit(solution)/shard_map/tile_start/pallas_call | solution.py:122
  65.6 36.4 %all_to_all.40.parts_ref = f32[32,72,128]{2,1,0:T(8,128)} all-to-all(f32[32,72,128]{2,1,0:T(8,128)} %tile_start.1), channel_id=1, replica_groups=mesh['row'=8,'col'=32] {'col'}, dimensions={0} | all-to-all | bytes 2359296 | tf_op jit(solution)/shard_map/all_to_all | solution.py:207
  102.0 2.2 start_update.1
  104.3 24.3 %all_to_all.41.rows_ref = bf16[32,80,128]{2,1,0:T(8,128)(2,1)} all-to-all(bf16[32,80,128]{2,1,0:T(8,128)(2,1)} %get-tuple-element.12), channel_id=1, replica_groups=mesh['row'=8,'col'=32] {'col'}, dimensions={0} | all-to-all | bytes 1310720 | tf_op jit(solution)/shard_map/all_to_all | solution.py:207
  128.5 14.7 %tile_pass.3 = f32[32,64,128]{2,1,0:T(8,128)} custom-call(s32[40]{0:T(128)} %bitcast.11, s32[40]{0:T(128)} %bitcast.15, bf16[40,256,256]{2,1,0:T(8,128)(2,1)} %scale_rates.1.rates_hbm, bf16[32,80,128]{2,1,0:T(8,128)(2,1)} %all_to_all.41.rows_ref, bf16[8192,128]{1,0:T(8,128)(2,1)} %all-gather.2.cloned.1.call-done.panel_ref), custom_call_target="tpu_custom_call" | custom-call | tf_op jit(solution)/shard_map/tile_pass/pallas_call | solution.py:122
  143.2 5.6 %all-to-all-start.3 = ((f32[32,64,128]{2,1,0:T(8,128)}), f32[32,64,128]{2,1,0:T(8,128)S(1)}, u32[]{:S(2)}, u32[]{:S(2)}) async-start(f32[32,64,128]{2,1,0:T(8,128)} %tile_pass.3), calls=%async_computation.3 | async-start | bytes 2097152 | tf_op jit(solution)/shard_map/all_to_all | solution.py:207
  148.8 0.9 slice_convert_fusion
  149.7 0.6 select_add_fusion.shift_ref
  150.4 24.4 %all-to-all-done.3.parts_ref = f32[32,64,128]{2,1,0:T(8,128)S(1)} async-done(((f32[32,64,128]{2,1,0:T(8,128)}), f32[32,64,128]{2,1,0:T(8,128)S(1)}, u32[]{:S(2)}, u32[]{:S(2)}) %all-to-all-start.3) | async-done | bytes 1048608 | tf_op jit(solution)/shard_map/all_to_all | solution.py:207
  174.8 0.0 copy-start.1
  174.8 1.0 copy-done.1
  175.8 2.5 update.2
  178.3 20.0 %all_to_all.42.rows_ref = bf16[32,64,128]{2,1,0:T(8,128)(2,1)} all-to-all(bf16[32,64,128]{2,1,0:T(8,128)(2,1)} %get-tuple-element.14), channel_id=1, replica_groups=mesh['row'=8,'col'=32] {'col'}, dimensions={0} | all-to-all | bytes 1048576 | tf_op jit(solution)/shard_map/all_to_all | solution.py:207
  198.3 14.7 %tile_pass.4 = f32[32,64,128]{2,1,0:T(8,128)} custom-call(s32[40]{0:T(128)} %bitcast.12, s32[40]{0:T(128)} %bitcast.16, bf16[40,256,256]{2,1,0:T(8,128)(2,1)} %scale_rates.1.rates_hbm, bf16[32,64,128]{2,1,0:T(8,128)(2,1)} %all_to_all.42.rows_ref, bf16[8192,128]{1,0:T(8,128)(2,1)} %all-gather.2.cloned.1.call-done.panel_ref), custom_call_target="tpu_custom_call" | custom-call | tf_op jit(solution)/shard_map/tile_pass/pallas_call | solution.py:122
  213.0 30.8 %all_to_all.43.parts_ref = f32[32,64,128]{2,1,0:T(8,128)} all-to-all(f32[32,64,128]{2,1,0:T(8,128)} %tile_pass.4), channel_id=1, replica_groups=mesh['row'=8,'col'=32] {'col'}, dimensions={0} | all-to-all | bytes 2097152 | tf_op jit(solution)/shard_map/all_to_all | solution.py:207
  243.8 2.5 update.3
  246.3 19.0 %all_to_all.44.rows_ref = bf16[32,64,128]{2,1,0:T(8,128)(2,1)} all-to-all(bf16[32,64,128]{2,1,0:T(8,128)(2,1)} %get-tuple-element.18), channel_id=1, replica_groups=mesh['row'=8,'col'=32] {'col'}, dimensions={0} | all-to-all | bytes 1048576 | tf_op jit(solution)/shard_map/all_to_all | solution.py:207
  265.4 14.6 %tile_pass.5 = f32[32,64,128]{2,1,0:T(8,128)} custom-call(s32[40]{0:T(128)} %bitcast.13, s32[40]{0:T(128)} %bitcast.17, bf16[40,256,256]{2,1,0:T(8,128)(2,1)} %scale_rates.1.rates_hbm, bf16[32,64,128]{2,1,0:T(8,128)(2,1)} %all_to_all.44.rows_ref, bf16[8192,128]{1,0:T(8,128)(2,1)} %all-gather.2.cloned.1.call-done.panel_ref), custom_call_target="tpu_custom_call" | custom-call | tf_op jit(solution)/shard_map/tile_pass/pallas_call | solution.py:122
  280.0 29.5 %all_to_all.45.parts_ref = f32[32,64,128]{2,1,0:T(8,128)} all-to-all(f32[32,64,128]{2,1,0:T(8,128)} %tile_pass.5), channel_id=1, replica_groups=mesh['row'=8,'col'=32] {'col'}, dimensions={0} | all-to-all | bytes 2097152 | tf_op jit(solution)/shard_map/all_to_all | solution.py:207
  309.5 2.2 update_last.1
  (2 shorter events, 0.0 us)
Async XLA Ops:
  7.2 33.4 %all-gather.2.cloned.1.call-start = ((), (), s32[]{:S(2)}) async-start(), calls=%async_computation.8 | async-start | bytes 2359296 | tf_op jit(solution)/shard_map/all_gather | solution.py:215
  9.9 39.7 %all-to-all-start = ((bf16[32,128,128]{2,1,0:T(8,128)(2,1)}), bf16[32,128,128]{2,1,0:T(8,128)(2,1)S(1)}, u32[]{:S(2)}, u32[]{:S(2)}) async-start(bf16[32,128,128]{2,1,0:T(8,128)(2,1)} %broadcast_in_dim.2), calls=%async_computation | async-start | bytes 2097152 | tf_op jit(solution)/shard_map/all_to_all | solution.py:207
  49.6 1.1 copy-start
  143.2 31.6 %all-to-all-start.3 = ((f32[32,64,128]{2,1,0:T(8,128)}), f32[32,64,128]{2,1,0:T(8,128)S(1)}, u32[]{:S(2)}, u32[]{:S(2)}) async-start(f32[32,64,128]{2,1,0:T(8,128)} %tile_pass.3), calls=%async_computation.3 | async-start | bytes 2097152 | tf_op jit(solution)/shard_map/all_to_all | solution.py:207
  174.8 1.0 copy-start.1
Sparse Core Ops, SparseCore 0:
  9.9 30.6 all-gather.1

commit v2 on v1

--- a/solution.py
+++ b/solution.py
@@ -10,7 +10,9 @@
 RANK = 128
 TILE = 256
 ITERS = 3
-GRAM_PAD = 8
+CODE_ROWS = 8
+START_ROWS = 16
+CODE_TOP = 32704.0
 GRAM_PARTS = 16
 
 confidence = 40.0
@@ -18,7 +20,7 @@
 
 bf16 = jnp.bfloat16
 f32 = jnp.float32
-VMEM_LIMIT = 56 * 1024 * 1024
+VMEM_LIMIT = 24 * 1024 * 1024
 
 
 def params():
@@ -34,7 +36,7 @@
 
 def scale_rates(count, rates):
     slots = rates.shape[0]
-    step_slots = 4
+    step_slots = 8
     return pl.pallas_call(
         functools.partial(rate_kernel, step_slots),
         grid_spec=pltpu.PrefetchScalarGridSpec(
@@ -54,95 +56,174 @@
     return high, (x - high.astype(f32)).astype(bf16)
 
 
-def tile_kernel(first, n_peer, own, users_ref, items_ref, rates_hbm, rows_ref, panel_ref, *rest):
-    if first:
-        gram_ref, out_ref, rates, sems = rest
-    else:
-        out_ref, rates, sems = rest
+def power_of_two(power):
+    size = jnp.abs(power).astype(jnp.int32)
+    up = jnp.ones_like(power)
+    down = jnp.ones_like(power)
+    for bit in range(7):
+        held = (size & (1 << bit)) != 0
+        up = up * jnp.where(held, 2.0 ** (1 << bit), 1.0)
+        down = down * jnp.where(held, 2.0 ** -(1 << bit), 1.0)
+    return jnp.where(power < 0, down, up)
+
+
+def bound_power(block):
+    peak = jnp.max(jnp.abs(block), axis=0, keepdims=True)
+    return jnp.ceil(jnp.log2(jnp.clip(peak, 1e-30, 1e36)) + 1e-3)
+
+
+def whole(x):
+    return jnp.round(x).astype(jnp.int32)
+
+
+def tile_kernel(first, n_peer, own, pieces, users_ref, items_ref, rates_hbm, rows_ref, *rest):
+    panel_hbm = rest[:pieces]
+    out_ref, rates, panel, total, sems, panel_sems = rest[pieces:]
     chunks = sems.shape[0]
     per = rates.shape[0] // chunks
     peers = TILE // own
+    piece_rows = panel.shape[0] // pieces
 
     def copy(k):
         part = pl.ds(k * per, per)
         return pltpu.make_async_copy(rates_hbm.at[part], rates.at[part], sems.at[k])
 
+    def panel_copy(k):
+        part = pl.ds(k * piece_rows, piece_rows)
+        return pltpu.make_async_copy(panel_hbm[k], panel.at[part], panel_sems.at[k])
+
+    for k in range(pieces):
+        panel_copy(k).start()
     for k in range(chunks):
         copy(k).start()
+    if not first:
+        total[...] = jnp.zeros_like(total)
+    for k in range(pieces):
+        panel_copy(k).wait()
     if first:
-        gram = gram_ref[...]
+        gram = jnp.zeros((RANK, RANK), f32)
+        for k in range(pieces):
+            part = panel[k * piece_rows:(k + 1) * piece_rows]
+            gram += lax.dot_general(
+                part, part, (((0,), (0,)), ((), ())), preferred_element_type=f32
+            )
         gram_high, gram_low = split2(gram)
-        for p in range(n_peer):
-            high = rows_ref[p, :own]
-            low = rows_ref[p, own:2 * own]
+        for p in range(0, n_peer, peers):
+            high = rows_ref[p:p + peers, :own].reshape(TILE, RANK)
+            low = rows_ref[p:p + peers, own:2 * own].reshape(TILE, RANK)
             shift = jnp.dot(high, gram_high, preferred_element_type=f32)
             shift += jnp.dot(high, gram_low, preferred_element_type=f32)
             shift += jnp.dot(low, gram_high, preferred_element_type=f32)
-            out_ref[p, :own] = -shift
-            out_ref[p, own:own + 4] = gram[4 * p:4 * p + 4]
-            out_ref[p, own + 4:] = jnp.zeros((GRAM_PAD - 4, RANK), f32)
-    else:
-        out_ref[...] = jnp.zeros_like(out_ref)
-
-    def slot(s):
-        user = users_ref[s] * peers
-        item = pl.multiple_of(items_ref[s] * TILE, TILE)
-        block = panel_ref[pl.ds(item, TILE), :]
-        field = rows_ref[pl.ds(user, peers), :own].reshape(TILE, RANK)
-        scores = lax.dot_general(
-            field, block, (((1,), (1,)), ((), ())), preferred_element_type=f32
-        )
-        rate = rates[s].astype(f32)
-        if first:
-            coef = jnp.where(rate > 0, 1.0 + rate * (1.0 - scores), 0.0)
-        else:
-            coef = rate * scores
-        contrib = jnp.dot(coef.astype(bf16), block, preferred_element_type=f32)
-        out_ref[pl.ds(user, peers), :own] += contrib.reshape(peers, own, RANK)
+            total[p:p + peers] = -shift.reshape(peers, own, RANK)
+
+    def group(start):
+        slots = [start + j for j in range(per)]
+        users = [users_ref[s] * peers for s in slots]
+        blocks = [
+            panel[pl.ds(pl.multiple_of(items_ref[s] * TILE, TILE), TILE), :] for s in slots
+        ]
+        fields = [rows_ref[pl.ds(u, peers), :own].reshape(TILE, RANK) for u in users]
+        scores = [
+            lax.dot_general(
+                field, block, (((1,), (1,)), ((), ())), preferred_element_type=f32
+            )
+            for field, block in zip(fields, blocks)
+        ]
+        coefs = []
+        for s, score in zip(slots, scores):
+            rate = rates[s].astype(f32)
+            if first:
+                coef = jnp.where(rate > 0, 1.0 + rate * (1.0 - score), 0.0)
+            else:
+                coef = rate * score
+            coefs.append(coef.astype(bf16))
+        contribs = [
+            jnp.dot(coef, block, preferred_element_type=f32)
+            for coef, block in zip(coefs, blocks)
+        ]
+        for user, contrib in zip(users, contribs):
+            total[pl.ds(user, peers)] += contrib.reshape(peers, own, RANK)
 
     for k in range(chunks):
         copy(k).wait()
-
-        def pair(i, carry):
-            slot(k * per + 2 * i)
-            slot(k * per + 2 * i + 1)
-            return carry
-
-        lax.fori_loop(0, per // 2, pair, 0)
-
-
-def tile_pass(first, users, items, rates, rows, panel, own, gram=None):
+        group(k * per)
+
+    lead = out_ref.shape[1] - own
+    powers = jnp.concatenate([bound_power(total[p]) for p in range(n_peer)], axis=0)
+    factors = power_of_two(-powers) * CODE_TOP
+    if first:
+        gram_powers = jnp.concatenate(
+            [bound_power(gram[4 * p:4 * p + 4]) for p in range(n_peer)], axis=0
+        )
+        gram_factors = power_of_two(-gram_powers) * CODE_TOP
+    for p in range(n_peer):
+        out_ref[p, :own] = whole(total[p] * factors[p:p + 1]).astype(jnp.int16)
+        lines = [powers[p:p + 1].astype(jnp.int32)]
+        if first:
+            scaled = gram[4 * p:4 * p + 4] * gram_factors[p:p + 1]
+            gram_high = whole(scaled)
+            gram_low = whole((scaled - gram_high.astype(f32)) * CODE_TOP)
+            lines += [gram_powers[p:p + 1].astype(jnp.int32), gram_high, gram_low]
+        filled = sum(line.shape[0] for line in lines)
+        lines.append(jnp.zeros((lead - filled, RANK), jnp.int32))
+        out_ref[p, own:] = jnp.concatenate(lines, axis=0).astype(jnp.int16)
+
+
+def tile_pass(first, users, items, rates, rows, panel, own):
     n_peer = rows.shape[0]
     slots = rates.shape[0]
     chunks = 5
     vmem = pl.BlockSpec(memory_space=pltpu.VMEM)
     smem = pl.BlockSpec(memory_space=pltpu.SMEM)
-    out_rows = own + (GRAM_PAD if first else 0)
-    operands = (users, items, rates, rows, panel) + ((gram,) if first else ())
+    hbm = pl.BlockSpec(memory_space=pl.ANY)
+    pieces = len(panel)
     return pl.pallas_call(
-        functools.partial(tile_kernel, first, n_peer, own),
-        in_specs=[smem, smem, pl.BlockSpec(memory_space=pl.ANY)] + [vmem] * (len(operands) - 3),
+        functools.partial(tile_kernel, first, n_peer, own, pieces),
+        in_specs=[smem, smem, hbm, vmem] + [hbm] * pieces,
         out_specs=vmem,
-        out_shape=jax.ShapeDtypeStruct((n_peer, out_rows, RANK), f32),
+        out_shape=jax.ShapeDtypeStruct((n_peer, own + (START_ROWS if first else CODE_ROWS), RANK), jnp.int16),
         scratch_shapes=[
             pltpu.VMEM((slots, TILE, TILE), bf16),
+            pltpu.VMEM((pieces * panel[0].shape[0], RANK), bf16),
+            pltpu.VMEM((n_peer, own, RANK), f32),
             pltpu.SemaphoreType.DMA((chunks,)),
+            pltpu.SemaphoreType.DMA((pieces,)),
         ],
         compiler_params=params(),
         name="tile_start" if first else "tile_pass",
-    )(*operands)
+    )(users, items, rates, rows, *panel)
+
+
+def code_lines(parts_ref, own):
+    return [parts_ref[p, own:].astype(f32) for p in range(parts_ref.shape[0])]
+
+
+def scales(lines, row):
+    powers = jnp.concatenate([line[row:row + 1] for line in lines], axis=0)
+    return power_of_two(powers) * (1.0 / CODE_TOP)
+
+
+def decode_sum(parts_ref, own, lines):
+    scale = scales(lines, 0)
+    image = jnp.zeros((own, RANK), f32)
+    for p in range(parts_ref.shape[0]):
+        image += parts_ref[p, :own].astype(f32) * scale[p:p + 1]
+    return image
 
 
 def start_update_kernel(own, parts_ref, prior_ref, residual_ref, sent_ref):
-    total = jnp.sum(parts_ref[...], axis=0)
-    residual = total[:own] - ridge_term * prior_ref[...]
+    lines = code_lines(parts_ref, own)
+    residual = decode_sum(parts_ref, own, lines) - ridge_term * prior_ref[...]
     residual_ref[...] = residual
-    gram = total[own:]
+    gram = jnp.zeros((4, RANK), f32)
+    scale = scales(lines, 1)
+    for p, line in enumerate(lines):
+        gram += (line[2:6] + line[6:10] * (1.0 / CODE_TOP)) * scale[p:p + 1]
     gram_high, rest = split2(gram)
     rest = gram - gram_high.astype(f32)
     gram_mid, gram_low = split2(rest)
     pack = jnp.concatenate(
-        [gram_high.astype(f32)[:4], gram_mid.astype(f32)[:4], gram_low.astype(f32)[:4],
+        [gram_high.astype(f32), gram_mid.astype(f32), gram_low.astype(f32),
          jnp.zeros((4, RANK), f32)], axis=0
     ).astype(bf16)
     sent = jnp.concatenate([residual.astype(bf16), pack], axis=0)
@@ -172,7 +253,8 @@
     shift = jnp.dot(
         direction, shift_ref[...], precision=lax.Precision.HIGHEST, preferred_element_type=f32
     )
-    image = jnp.sum(parts_ref[...].astype(f32), axis=0) + shift
+    own = direction.shape[0]
+    image = decode_sum(parts_ref, own, code_lines(parts_ref, own)) + shift
     norm_now = jnp.sum(residual * residual, axis=1, keepdims=True)
     step_size = norm_now / jnp.sum(direction * image, axis=1, keepdims=True)
     outs[0][...] = factors_ref[...] + step_size * direction
@@ -207,20 +289,36 @@
     return lax.all_to_all(blocks, "col", 0, 0, tiled=True)
 
 
+def gather_panel(shard, items, beside):
+    n_row = lax.axis_size("row")
+    me = lax.axis_index("row")
+    pair = [(r, r ^ 1) for r in range(n_row)]
+    mine = [shard]
+    for k in range(1, n_row // 2):
+        ring = [(r, (r + 2 * k) % n_row) for r in range(n_row)]
+        mine.append(lax.ppermute(shard, "row", ring))
+    mine, beside = lax.optimization_barrier((mine, beside))
+    pieces = []
+    for piece in mine:
+        pieces += [piece, lax.ppermute(piece, "row", pair)]
+    tiles = shard.shape[0] // TILE
+    owner = items // tiles
+    turn = (me // 2 - owner // 2) % (n_row // 2)
+    place = turn * 2 + (owner % 2 != me % 2).astype(items.dtype)
+    return pieces, place * tiles + items % tiles, beside
+
+
 def body(prior_factors, item_factors, user_tiles, item_tiles, tile_counts, ratings):
     users = user_tiles[0, 0]
     items = item_tiles[0, 0]
     own = prior_factors.shape[0]
     n_peer = lax.axis_size("col")
-    panel = lax.all_gather(item_factors, "row", axis=0, tiled=True)
     rates = scale_rates(tile_counts[0], ratings[0, 0])
+    panel, items, rates = gather_panel(item_factors, items, rates)
     high = lax.reduce_precision(prior_factors, 8, 7)
     rows = jnp.concatenate([high, prior_factors - high], axis=0).astype(bf16)
     rows = exchange(jnp.broadcast_to(rows[None], (n_peer,) + rows.shape))
-    gram = lax.dot_general(
-        panel, panel, (((0,), (0,)), ((), ())), preferred_element_type=f32
-    )
-    parts = exchange(tile_pass(True, users, items, rates, rows, panel, own, gram))
+    parts = exchange(tile_pass(True, users, items, rates, rows, panel, own))
     residual, sent = start_update(parts, prior_factors)
     direction = residual
     factors = prior_factors

time: 320 us -> 231 us (0.72)
  the two profiles are of different devices: /device:TPU:2 before, /device:TPU:24 now
where the time goes in v2:
time: 231 us
  blocking collectives  133 us (58%)
  waiting for transfers between devices  32.6 us (14%)
  Pallas kernels  26.8 us (12%)
  starting transfers between devices  20.8 us (9%)
  local copies, waits for them, and re-layouts  14.2 us (6%)
    all_to_all x6, blocking collectives, exchange(): return lax.all_to_all(blocks, 'col', 0, 0, tiled=True)  133 us
    all_to_all x2, waiting for transfers between devices, exchange(): return lax.all_to_all(blocks, 'col', 0, 0, tiled=True)  27.2 us
    pallas_call x4, Pallas kernels, tile_pass(): pl.pallas_call(functools.partial(tile_kernel, first, n_peer, own, pieces)...  22.6 us
    all_to_all x2, starting transfers between devices, exchange(): return lax.all_to_all(blocks, 'col', 0, 0, tiled=True)  16.2 us
    unnamed x26, local copies, waits for them, and re-layouts  12.9 us
  transfers between devices with their start and end apart: 9, of which 8 were waited for; matrix products, arithmetic and copies ran while one was open for 0% of the time, Pallas kernels for 0%

profile of v2, /device:TPU:24, one launch (start us, length us, event | category | flops | bytes accessed | tf_op | source)
XLA Modules:
  0.0 230.6 jit_solution(14711129211922492458)
XLA Ops:
  0.6 0.0 copy-start.5
  0.6 0.0 copy-start.10
  0.7 0.0 copy-start.9
  0.7 0.8 reduce-precision_convert_fusion
  1.5 1.2 broadcast_in_dim.2
  2.7 11.3 %all-to-all-start = ((bf16[32,128,128]{2,1,0:T(8,128)(2,1)}), bf16[32,128,128]{2,1,0:T(8,128)(2,1)S(1)}, u32[]{:S(2)}, u32[]{:S(2)}) async-start(bf16[32,128,128]{2,1,0:T(8,128)(2,1)} %broadcast_in_dim.2), calls=%async_computation | async-start | bytes 2097152 | tf_op jit(solution)/shard_map/all_to_all | solution.py:289
  14.0 1.3 collective-permute-start.1
  15.3 2.2 collective-permute-start
  17.5 0.0 collective-permute-start.2
  18.2 0.0 copy-start.4
  18.2 4.0 %copy-done.4 = s32[1,1,40,256,256]{4,3,2,1,0:T(8,128)S(1)} copy-done((s32[1,1,40,256,256]{4,3,2,1,0:T(8,128)S(1)}, s32[1,1,40,256,256]{4,3,2,1,0:T(8,128)}, u32[]{:S(2)}) %copy-start.4) | copy-done | bytes 10485784
  22.2 0.9 scale_rates.1.rates_hbm
  23.1 0.0 copy-start
  23.1 2.3 %copy-done = bf16[40,256,256]{2,1,0:T(8,128)(2,1)} copy-done((bf16[40,256,256]{2,1,0:T(8,128)(2,1)}, bf16[40,256,256]{2,1,0:T(8,128)(2,1)S(1)}, u32[]{:S(2)}) %copy-start) | copy-done | bytes 5242904
  25.4 0.0 collective-permute-done.1.rest_4_
  25.4 1.3 collective-permute-done.rest_2_
  26.8 2.4 %collective-permute-done.2.rest_6_ = bf16[1024,128]{1,0:T(8,128)(2,1)S(1)} collective-permute-done((bf16[1024,128]{1,0:T(8,128)(2,1)}, bf16[1024,128]{1,0:T(8,128)(2,1)S(1)}, u32[]{:S(2)}, u32[]{:S(2)}) %collective-permute-start.2) | collective-permute-done | bytes 262176 | tf_op jit(solution)/shard_map/ppermute | solution.py:299
  29.2 0.0 copy-done.5
  29.2 0.0 collective-permute-start.3
  29.2 0.5 collective-permute-start.4
  29.7 0.0 collective-permute-start.5
  29.7 0.5 collective-permute-start.6
  30.3 0.5 collective-permute-done.3.rest_1_
  30.7 0.4 collective-permute-done.4.rest_3_
  31.1 0.4 collective-permute-done.5.rest_5_
  31.5 0.4 collective-permute-done.6.rest_7_
  31.9 10.2 %all-to-all-done.rows_ref = bf16[32,128,128]{2,1,0:T(8,128)(2,1)S(1)} async-done(((bf16[32,128,128]{2,1,0:T(8,128)(2,1)}), bf16[32,128,128]{2,1,0:T(8,128)(2,1)S(1)}, u32[]{:S(2)}, u32[]{:S(2)}) %all-to-all-start) | async-done | bytes 1048608 | tf_op jit(solution)/shard_map/all_to_all | solution.py:289
  42.1 2.5 %copy-done.1 = bf16[40,256,256]{2,1,0:T(8,128)(2,1)S(1)} copy-done((bf16[40,256,256]{2,1,0:T(8,128)(2,1)S(1)}, bf16[40,256,256]{2,1,0:T(8,128)(2,1)}, u32[]{:S(2)}) %copy-start.1) | copy-done | bytes 5242904
  44.6 7.2 %tile_start.1 = s16[32,80,128]{2,1,0:T(8,128)(2,1)S(1)} custom-call(s32[40]{0:T(128)S(1)} %bitcast.21, s32[40]{0:T(128)S(1)} %fusion.1.items_ref, bf16[40,256,256]{2,1,0:T(8,128)(2,1)S(1)} %copy-done.1, bf16[32,128,128]{2,1,0:T(8,128)(2,1)S(1)} %all-to-all-done.rows_ref, bf16[1024,128]{1,0:T(8,128)(2,1)S(1)} %copy-done.5, ...), custom_call_target="tpu_custom_call" | custom-call | tf_op jit(solution)/shard_map/tile_start/pallas_call | solution.py:180
  51.8 24.7 %all_to_all.40.parts_ref = s16[32,80,128]{2,1,0:T(8,128)(2,1)S(1)} all-to-all(s16[32,80,128]{2,1,0:T(8,128)(2,1)S(1)} %tile_start.1), channel_id=1, replica_groups=mesh['row'=8,'col'=32] {'col'}, dimensions={0} | all-to-all | bytes 1310720 | tf_op jit(solution)/shard_map/all_to_all | solution.py:289
  76.5 0.3 start_update.1
  76.9 23.8 %all_to_all.41.rows_ref = bf16[32,80,128]{2,1,0:T(8,128)(2,1)S(1)} all-to-all(bf16[32,80,128]{2,1,0:T(8,128)(2,1)S(1)} %get-tuple-element.22), channel_id=1, replica_groups=mesh['row'=8,'col'=32] {'col'}, dimensions={0} | all-to-all | bytes 1310720 | tf_op jit(solution)/shard_map/all_to_all | solution.py:289
  100.7 5.1 %tile_pass.3 = s16[32,72,128]{2,1,0:T(8,128)(2,1)S(1)} custom-call(s32[40]{0:T(128)S(1)} %bitcast.22, s32[40]{0:T(128)S(1)} %fusion.1.items_ref, bf16[40,256,256]{2,1,0:T(8,128)(2,1)S(1)} %copy-done.2, bf16[32,80,128]{2,1,0:T(8,128)(2,1)S(1)} %all_to_all.41.rows_ref, bf16[1024,128]{1,0:T(8,128)(2,1)S(1)} %copy-done.5, ...), custom_call_target="tpu_custom_call" | custom-call | tf_op jit(solution)/shard_map/tile_pass/pallas_call | solution.py:180
  105.8 0.8 copy-done.6
  106.7 0.8 copy-done.7
  107.5 4.9 %all-to-all-start.3 = ((s16[32,72,128]{2,1,0:T(8,128)(2,1)}), s16[32,72,128]{2,1,0:T(8,128)(2,1)}, u32[]{:S(2)}, u32[]{:S(2)}) async-start(s16[32,72,128]{2,1,0:T(8,128)(2,1)} %copy-done.7), calls=%async_computation.3 | async-start | bytes 1179648 | tf_op jit(solution)/shard_map/all_to_all | solution.py:289
  112.4 0.9 slice_convert_fusion
  113.4 17.0 %all-to-all-done.3.parts_ref = s16[32,72,128]{2,1,0:T(8,128)(2,1)} async-done(((s16[32,72,128]{2,1,0:T(8,128)(2,1)}), s16[32,72,128]{2,1,0:T(8,128)(2,1)}, u32[]{:S(2)}, u32[]{:S(2)}) %all-to-all-start.3) | async-done | bytes 589856 | tf_op jit(solution)/shard_map/all_to_all | solution.py:289
  130.4 1.5 update.2
  131.9 20.8 %all_to_all.42.rows_ref = bf16[32,64,128]{2,1,0:T(8,128)(2,1)S(1)} all-to-all(bf16[32,64,128]{2,1,0:T(8,128)(2,1)S(1)} %get-tuple-element.24), channel_id=1, replica_groups=mesh['row'=8,'col'=32] {'col'}, dimensions={0} | all-to-all | bytes 1048576 | tf_op jit(solution)/shard_map/all_to_all | solution.py:289
  152.8 2.5 %copy-done.3 = bf16[40,256,256]{2,1,0:T(8,128)(2,1)S(1)} copy-done((bf16[40,256,256]{2,1,0:T(8,128)(2,1)S(1)}, bf16[40,256,256]{2,1,0:T(8,128)(2,1)}, u32[]{:S(2)}) %copy-start.3) | copy-done | bytes 5242904
  155.3 5.1 %tile_pass.4 = s16[32,72,128]{2,1,0:T(8,128)(2,1)S(1)} custom-call(s32[40]{0:T(128)S(1)} %bitcast.23, s32[40]{0:T(128)S(1)} %fusion.1.items_ref, bf16[40,256,256]{2,1,0:T(8,128)(2,1)S(1)} %copy-done.3, bf16[32,64,128]{2,1,0:T(8,128)(2,1)S(1)} %all_to_all.42.rows_ref, bf16[1024,128]{1,0:T(8,128)(2,1)S(1)} %copy-done.5, ...), custom_call_target="tpu_custom_call" | custom-call | tf_op jit(solution)/shard_map/tile_pass/pallas_call | solution.py:180
  160.4 21.8 %all_to_all.43.parts_ref = s16[32,72,128]{2,1,0:T(8,128)(2,1)S(1)} all-to-all(s16[32,72,128]{2,1,0:T(8,128)(2,1)S(1)} %tile_pass.4), channel_id=1, replica_groups=mesh['row'=8,'col'=32] {'col'}, dimensions={0} | all-to-all | bytes 1179648 | tf_op jit(solution)/shard_map/all_to_all | solution.py:289
  182.2 0.5 update.3
  182.7 20.6 %all_to_all.44.rows_ref = bf16[32,64,128]{2,1,0:T(8,128)(2,1)S(1)} all-to-all(bf16[32,64,128]{2,1,0:T(8,128)(2,1)S(1)} %get-tuple-element.28), channel_id=1, replica_groups=mesh['row'=8,'col'=32] {'col'}, dimensions={0} | all-to-all | bytes 1048576 | tf_op jit(solution)/shard_map/all_to_all | solution.py:289
  203.2 5.1 %tile_pass.5 = s16[32,72,128]{2,1,0:T(8,128)(2,1)S(1)} custom-call(s32[40]{0:T(128)S(1)} %bitcast.24, s32[40]{0:T(128)S(1)} %fusion.1.items_ref, bf16[40,256,256]{2,1,0:T(8,128)(2,1)S(1)} %bitcast.19, bf16[32,64,128]{2,1,0:T(8,128)(2,1)S(1)} %all_to_all.44.rows_ref, bf16[1024,128]{1,0:T(8,128)(2,1)S(1)} %copy-done.5, ...), custom_call_target="tpu_custom_call" | custom-call | tf_op jit(solution)/shard_map/tile_pass/pallas_call | solution.py:180
  208.4 21.3 %all_to_all.45.parts_ref = s16[32,72,128]{2,1,0:T(8,128)(2,1)S(1)} all-to-all(s16[32,72,128]{2,1,0:T(8,128)(2,1)S(1)} %tile_pass.5), channel_id=1, replica_groups=mesh['row'=8,'col'=32] {'col'}, dimensions={0} | all-to-all | bytes 1179648 | tf_op jit(solution)/shard_map/all_to_all | solution.py:289
  229.6 1.0 update_last.1
  (19 shorter events, 0.1 us)
Async XLA Ops:
  0.6 28.6 %copy-start.5 = (bf16[1024,128]{1,0:T(8,128)(2,1)S(1)}, bf16[1024,128]{1,0:T(8,128)(2,1)}, u32[]{:S(2)}) copy-start(bf16[1024,128]{1,0:T(8,128)(2,1)} %rest_0_.3) | copy-start | bytes 786436
  0.6 29.6 %copy-start.10 = (s32[1,1,40]{2,1,0:T(1,128)S(1)}, s32[1,1,40]{2,1,0:T(1,128)}, u32[]{:S(2)}) copy-start(s32[1,1,40]{2,1,0:T(1,128)} %param.9) | copy-start | bytes 484
  0.7 41.5 %copy-start.9 = (s32[1,1,40]{2,1,0:T(1,128)S(1)}, s32[1,1,40]{2,1,0:T(1,128)}, u32[]{:S(2)}) copy-start(s32[1,1,40]{2,1,0:T(1,128)} %param.8) | copy-start | bytes 484
  2.7 39.4 %all-to-all-start = ((bf16[32,128,128]{2,1,0:T(8,128)(2,1)}), bf16[32,128,128]{2,1,0:T(8,128)(2,1)S(1)}, u32[]{:S(2)}, u32[]{:S(2)}) async-start(bf16[32,128,128]{2,1,0:T(8,128)(2,1)} %broadcast_in_dim.2), calls=%async_computation | async-start | bytes 2097152 | tf_op jit(solution)/shard_map/all_to_all | solution.py:289
  14.0 11.4 %collective-permute-start.1 = (bf16[1024,128]{1,0:T(8,128)(2,1)}, bf16[1024,128]{1,0:T(8,128)(2,1)S(1)}, u32[]{:S(2)}, u32[]{:S(2)}) collective-permute-start(bf16[1024,128]{1,0:T(8,128)(2,1)} %rest_0_.3), channel_id=1, source_target_pairs={{0,128},{32,160},{64,192},{96,224},{128,0},{160,32},{192,64},{224,... | collective-permute-start | bytes 786440 | tf_op jit(solution)/shard_map/ppermute | solution.py:299
  15.3 11.4 %collective-permute-start = (bf16[1024,128]{1,0:T(8,128)(2,1)}, bf16[1024,128]{1,0:T(8,128)(2,1)S(1)}, u32[]{:S(2)}, u32[]{:S(2)}) collective-permute-start(bf16[1024,128]{1,0:T(8,128)(2,1)} %rest_0_.3), channel_id=1, source_target_pairs={{0,64},{32,96},{64,128},{96,160},{128,192},{160,224},{192,0},{224,... | collective-permute-start | bytes 786440 | tf_op jit(solution)/shard_map/ppermute | solution.py:299
  17.5 11.7 %collective-permute-start.2 = (bf16[1024,128]{1,0:T(8,128)(2,1)}, bf16[1024,128]{1,0:T(8,128)(2,1)S(1)}, u32[]{:S(2)}, u32[]{:S(2)}) collective-permute-start(bf16[1024,128]{1,0:T(8,128)(2,1)} %rest_0_.3), channel_id=1, source_target_pairs={{0,192},{32,224},{64,0},{96,32},{128,64},{160,96},{192,128},{224,1... | collective-permute-start | bytes 786440 | tf_op jit(solution)/shard_map/ppermute | solution.py:299
  18.2 4.0 %copy-start.4 = (s32[1,1,40,256,256]{4,3,2,1,0:T(8,128)S(1)}, s32[1,1,40,256,256]{4,3,2,1,0:T(8,128)}, u32[]{:S(2)}) copy-start(s32[1,1,40,256,256]{4,3,2,1,0:T(8,128)} %param.11) | copy-start | bytes 31457284
  22.2 54.4 %copy-start.8 = (f32[64,128]{1,0:T(8,128)S(1)}, f32[64,128]{1,0:T(8,128)}, u32[]{:S(2)}) copy-start(f32[64,128]{1,0:T(8,128)} %factors_ref.1) | copy-start | bytes 98308
  23.1 2.3 %copy-start = (bf16[40,256,256]{2,1,0:T(8,128)(2,1)}, bf16[40,256,256]{2,1,0:T(8,128)(2,1)S(1)}, u32[]{:S(2)}) copy-start(bf16[40,256,256]{2,1,0:T(8,128)(2,1)S(1)} %scale_rates.1.rates_hbm) | copy-start | bytes 15728644
  29.2 1.5 collective-permute-start.3
  29.2 1.9 collective-permute-start.4
  29.7 1.8 collective-permute-start.5
  29.7 2.1 collective-permute-start.6
  42.1 2.5 %copy-start.1 = (bf16[40,256,256]{2,1,0:T(8,128)(2,1)S(1)}, bf16[40,256,256]{2,1,0:T(8,128)(2,1)}, u32[]{:S(2)}) copy-start(bf16[40,256,256]{2,1,0:T(8,128)(2,1)} %copy-done) | copy-start | bytes 15728644
  44.6 56.1 %copy-start.2 = (bf16[40,256,256]{2,1,0:T(8,128)(2,1)S(1)}, bf16[40,256,256]{2,1,0:T(8,128)(2,1)}, u32[]{:S(2)}) copy-start(bf16[40,256,256]{2,1,0:T(8,128)(2,1)} %copy-done) | copy-start | bytes 15728644
  105.8 0.8 copy-start.6
  106.7 0.8 copy-start.7
  107.5 95.8 %slice-start = ((s8[5242880]{0:T(1024)(128)(4,1)}), s8[1048576]{0:T(1024)(128)(4,1)S(1)}, s32[]{:S(2)}) async-start(s8[5242880]{0:T(1024)(128)(4,1)} %bitcast.18), calls=%async_computation.8 | async-start | bytes 2097152
  107.5 22.9 %all-to-all-start.3 = ((s16[32,72,128]{2,1,0:T(8,128)(2,1)}), s16[32,72,128]{2,1,0:T(8,128)(2,1)}, u32[]{:S(2)}, u32[]{:S(2)}) async-start(s16[32,72,128]{2,1,0:T(8,128)(2,1)} %copy-done.7), calls=%async_computation.3 | async-start | bytes 1179648 | tf_op jit(solution)/shard_map/all_to_all | solution.py:289
  152.8 2.5 %copy-start.3 = (bf16[40,256,256]{2,1,0:T(8,128)(2,1)S(1)}, bf16[40,256,256]{2,1,0:T(8,128)(2,1)}, u32[]{:S(2)}) copy-start(bf16[40,256,256]{2,1,0:T(8,128)(2,1)} %copy-done) | copy-start | bytes 15728644
  155.3 48.0 %slice-start.1 = ((s8[5242880]{0:T(1024)(128)(4,1)}), s8[4194304]{0:T(1024)(128)(4,1)S(1)}, s32[]{:S(2)}) async-start(s8[5242880]{0:T(1024)(128)(4,1)} %bitcast.18), calls=%async_computation.9 | async-start | bytes 8388608

commit v3 on v2

v3 whole, which is shorter than its diff:
```python
import functools

import jax
import jax.numpy as jnp
from jax import lax
from jax.experimental import pallas as pl
from jax.experimental.pallas import tpu as pltpu
from jax.sharding import PartitionSpec as P

RANK = 128
TILE = 256
ITERS = 3
CODE_ROWS = 8
START_ROWS = 16
CODE_TOP = 32704.0
GRAM_ROWS = 16

confidence = 40.0
ridge_term = 0.1

bf16 = jnp.bfloat16
f32 = jnp.float32
VMEM_LIMIT = 24 * 1024 * 1024
START_LIMIT = 46 * 1024 * 1024


def params(limit=VMEM_LIMIT):
    return pltpu.CompilerParams(vmem_limit_bytes=limit)


def power_of_two(power):
    size = jnp.abs(power).astype(jnp.int32)
    up = jnp.ones_like(power)
    down = jnp.ones_like(power)
    for bit in range(7):
        held = (size & (1 << bit)) != 0
        up = up * jnp.where(held, 2.0 ** (1 << bit), 1.0)
        down = down * jnp.where(held, 2.0 ** -(1 << bit), 1.0)
    return jnp.where(power < 0, down, up)


def bound_power(block):
    peak = jnp.max(jnp.abs(block), axis=0, keepdims=True)
    return jnp.ceil(jnp.log2(jnp.clip(peak, 1e-30, 1e36)) + 1e-3)


def whole(x):
    return jnp.round(x).astype(jnp.int32)


def tile_kernel(first, n_peer, own, pieces, users_ref, items_ref, rates, rows_ref, *rest):
    if first:
        count_ref, gram_ref = rest[:2]
        panel_hbm = rest[2:2 + pieces]
        out_ref, panel, scaled_rates, total, panel_sems, ratings, rate_sems = rest[2 + pieces:]
        rates_hbm, rates = rates, ratings
    else:
        panel, out_ref, total = rest
    per = 8
    peers = TILE // own

    def panel_copy(k):
        part = pl.ds(k * (panel.shape[0] // pieces), panel.shape[0] // pieces)
        return pltpu.make_async_copy(panel_hbm[k], panel.at[part], panel_sems.at[k])

    def rate_copy(k):
        part = pl.ds(k * per, per)
        return pltpu.make_async_copy(rates_hbm.at[part], rates.at[part], rate_sems.at[k])

    if first:
        for k in range(pieces):
            panel_copy(k).start()
        for k in range(rates.shape[0] // per):
            rate_copy(k).start()
    total[...] = jnp.zeros_like(total)
    if first:
        for k in range(pieces):
            panel_copy(k).wait()

    def group(start):
        slots = [start + j for j in range(per)]
        users = [users_ref[s] * peers for s in slots]
        blocks = [
            panel[pl.ds(pl.multiple_of(items_ref[s] * TILE, TILE), TILE), :] for s in slots
        ]
        fields = [rows_ref[pl.ds(u, peers), :own].reshape(TILE, RANK) for u in users]
        scores = [
            lax.dot_general(
                field, block, (((1,), (1,)), ((), ())), preferred_element_type=f32
            )
            for field, block in zip(fields, blocks)
        ]
        coefs = []
        for s, score in zip(slots, scores):
            rate = rates[s].astype(f32)
            if first:
                rate = rate * jnp.where(s < count_ref[0], confidence, 0.0)
                scaled_rates[s] = rate.astype(bf16)
                coef = jnp.where(rate > 0, 1.0 + rate * (1.0 - score), 0.0)
            else:
                coef = rate * score
            coefs.append(coef.astype(bf16))
        contribs = [
            jnp.dot(coef, block, preferred_element_type=f32)
            for coef, block in zip(coefs, blocks)
        ]
        for user, contrib in zip(users, contribs):
            total[pl.ds(user, peers)] += contrib.reshape(peers, own, RANK)

    for k in range(rates.shape[0] // per):
        if first:
            rate_copy(k).wait()
        group(k * per)

    lead = out_ref.shape[1] - own
    powers = jnp.concatenate([bound_power(total[p]) for p in range(n_peer)], axis=0)
    factors = power_of_two(-powers) * CODE_TOP
    extra = [jnp.zeros((lead - 1, RANK), jnp.int32)]
    if first:
        gram = gram_ref[...]
        gram_power = bound_power(gram)
        scaled = gram * (power_of_two(-gram_power) * CODE_TOP)
        gram_high = whole(scaled)
        gram_low = whole((scaled - gram_high.astype(f32)) * CODE_TOP)
        extra = [gram_power.astype(jnp.int32), gram_high, gram_low,
                 jnp.zeros((lead - 2 - 2 * gram.shape[0], RANK), jnp.int32)]
    for p in range(n_peer):
        out_ref[p, :own] = whole(total[p] * factors[p:p + 1]).astype(jnp.int16)
        lines = [powers[p:p + 1].astype(jnp.int32)] + extra
        out_ref[p, own:] = jnp.concatenate(lines, axis=0).astype(jnp.int16)


def tile_pass(first, users, items, rates, rows, panel, own, count=None, gram=None):
    n_peer = rows.shape[0]
    vmem = pl.BlockSpec(memory_space=pltpu.VMEM)
    smem = pl.BlockSpec(memory_space=pltpu.SMEM)
    hbm = pl.BlockSpec(memory_space=pl.ANY)
    code_rows = own + (START_ROWS if first else CODE_ROWS)
    out_shape = [jax.ShapeDtypeStruct((n_peer, code_rows, RANK), jnp.int16)]
    scratch = [pltpu.VMEM((n_peer, own, RANK), f32)]
    specs = [smem, smem, vmem, vmem]
    operands = [users, items, rates, rows]
    pieces = 0
    if first:
        pieces = len(panel)
        out_shape.append(jax.ShapeDtypeStruct((pieces * panel[0].shape[0], RANK), bf16))
        out_shape.append(jax.ShapeDtypeStruct(rates.shape, bf16))
        scratch.append(pltpu.SemaphoreType.DMA((pieces,)))
        scratch.append(pltpu.VMEM(rates.shape, rates.dtype))
        scratch.append(pltpu.SemaphoreType.DMA((rates.shape[0] // 8,)))
        specs[2] = hbm
        specs += [smem, vmem] + [hbm] * pieces
        operands += [count, gram] + list(panel)
    else:
        specs.append(vmem)
        operands.append(panel)
    out = pl.pallas_call(
        functools.partial(tile_kernel, first, n_peer, own, pieces),
        in_specs=specs,
        out_specs=[vmem] * len(out_shape),
        out_shape=out_shape,
        scratch_shapes=scratch,
        compiler_params=params(START_LIMIT if first else VMEM_LIMIT),
        name="tile_start" if first else "tile_pass",
    )(*operands)
    return out if first else out[0]


def code_lines(parts_ref, own):
    return [parts_ref[p, own:].astype(f32) for p in range(parts_ref.shape[0])]


def scales(lines, row):
    powers = jnp.concatenate([line[row:row + 1] for line in lines], axis=0)
    return power_of_two(powers) * (1.0 / CODE_TOP)


def decode_sum(parts_ref, own, lines):
    scale = scales(lines, 0)
    image = jnp.zeros((own, RANK), f32)
    for p in range(parts_ref.shape[0]):
        image += parts_ref[p, :own].astype(f32) * scale[p:p + 1]
    return image


def start_update_kernel(own, parts_ref, prior_ref, residual_ref, shift_ref, sent_ref):
    lines = code_lines(parts_ref, own)
    scale = scales(lines, 1)
    gram = jnp.concatenate(
        [
            (line[2:6] + line[6:10] * (1.0 / CODE_TOP)) * scale[p:p + 1]
            for p, line in enumerate(lines)
        ],
        axis=0,
    )
    row = lax.broadcasted_iota(jnp.int32, gram.shape, 0)
    column = lax.broadcasted_iota(jnp.int32, gram.shape, 1)
    shifted = gram + jnp.where(row == column, ridge_term, 0.0)
    shift_ref[...] = shifted
    shift = jnp.dot(
        prior_ref[...], shifted, precision=lax.Precision.HIGHEST, preferred_element_type=f32
    )
    residual = decode_sum(parts_ref, own, lines) - shift
    residual_ref[...] = residual
    sent_ref[...] = jnp.broadcast_to(residual.astype(bf16)[None], sent_ref.shape)


def start_update(parts, prior):
    n_peer = parts.shape[0]
    own = prior.shape[0]
    vmem = pl.BlockSpec(memory_space=pltpu.VMEM)
    return pl.pallas_call(
        functools.partial(start_update_kernel, own),
        in_specs=[vmem] * 2,
        out_specs=[vmem] * 3,
        out_shape=[
            jax.ShapeDtypeStruct(prior.shape, f32),
            jax.ShapeDtypeStruct((RANK, RANK), f32),
            jax.ShapeDtypeStruct((n_peer, own, RANK), bf16),
        ],
        compiler_params=params(),
        name="start_update",
    )(parts, prior)


def prepare_kernel(own, prior_ref, shard_ref, other_ref, sent_ref):
    n_peer = sent_ref.shape[0]
    gram = jnp.zeros((RANK, RANK), f32)
    for ref in (shard_ref, other_ref):
        shard = ref[...]
        gram += lax.dot_general(
            shard, shard, (((0,), (0,)), ((), ())), preferred_element_type=f32
        )
    parts = []
    rest = gram
    for _ in range(3):
        part = rest.astype(bf16).astype(f32)
        parts.append(part)
        rest = rest - part
    prior = prior_ref[...].astype(bf16)
    rows = RANK // n_peer
    filler = jnp.zeros((GRAM_ROWS - 3 * rows, RANK), f32)
    for p in range(n_peer):
        sent_ref[p, :own] = prior
        lines = [part[rows * p:rows * p + rows] for part in parts] + [filler]
        sent_ref[p, own:] = jnp.concatenate(lines, axis=0).astype(bf16)


def prepare(prior, shard, other, n_peer):
    own = prior.shape[0]
    vmem = pl.BlockSpec(memory_space=pltpu.VMEM)
    return pl.pallas_call(
        functools.partial(prepare_kernel, own),
        in_specs=[vmem] * 3,
        out_specs=vmem,
        out_shape=jax.ShapeDtypeStruct((n_peer, own + GRAM_ROWS, RANK), bf16),
        compiler_params=params(),
        name="prepare",
    )(prior, shard, other)


def update_kernel(last, parts_ref, shift_ref, factors_ref, residual_ref, direction_ref, *outs):
    direction = direction_ref[...]
    residual = residual_ref[...]
    shift = jnp.dot(
        direction, shift_ref[...], precision=lax.Precision.HIGHEST, preferred_element_type=f32
    )
    own = direction.shape[0]
    image = decode_sum(parts_ref, own, code_lines(parts_ref, own)) + shift
    norm_now = jnp.sum(residual * residual, axis=1, keepdims=True)
    step_size = norm_now / jnp.sum(direction * image, axis=1, keepdims=True)
    outs[0][...] = factors_ref[...] + step_size * direction
    residual = residual - step_size * image
    outs[1][...] = residual
    if not last:
        norm_next = jnp.sum(residual * residual, axis=1, keepdims=True)
        direction = residual + norm_next / norm_now * direction
        outs[2][...] = direction
        outs[3][...] = jnp.broadcast_to(direction.astype(bf16)[None], outs[3].shape)


def update(last, parts, shifted, factors, residual, direction):
    n_peer = parts.shape[0]
    own = factors.shape[0]
    vmem = pl.BlockSpec(memory_space=pltpu.VMEM)
    state = jax.ShapeDtypeStruct(factors.shape, f32)
    shapes = [state] * 2
    if not last:
        shapes += [state, jax.ShapeDtypeStruct((n_peer, own, RANK), bf16)]
    return pl.pallas_call(
        functools.partial(update_kernel, last),
        in_specs=[vmem] * 5,
        out_specs=[vmem] * len(shapes),
        out_shape=shapes,
        compiler_params=params(),
        name="update_last" if last else "update",
    )(parts, shifted, factors, residual, direction)


def exchange(blocks):
    return lax.all_to_all(blocks, "col", 0, 0, tiled=True)


def along_y(x):
    n_row = lax.axis_size("row")
    return [x] + [
        lax.ppermute(x, "row", [(r, (r + 2 * k) % n_row) for r in range(n_row)])
        for k in range(1, n_row // 2)
    ]


def panel_places(items, tiles):
    n_row = lax.axis_size("row")
    me = lax.axis_index("row")
    owner = items // tiles
    turn = (me // 2 - owner // 2) % (n_row // 2)
    place = turn * 2 + (owner % 2 != me % 2).astype(items.dtype)
    return place * tiles + items % tiles


def body(prior_factors, item_factors, user_tiles, item_tiles, tile_counts, ratings):
    users = user_tiles[0, 0]
    own = prior_factors.shape[0]
    n_peer = lax.axis_size("col")
    items = panel_places(item_tiles[0, 0], item_factors.shape[0] // TILE)
    swap = [(r, r ^ 1) for r in range(lax.axis_size("row"))]
    other = lax.ppermute(item_factors, "row", swap)
    mine = along_y(item_factors)
    sent = prepare(prior_factors, item_factors, other, n_peer)

    leads = lax.axis_index("row") % 2 == 0
    rows = lax.cond(leads, exchange, lambda x: x, sent)
    rows, mine = lax.optimization_barrier((rows, mine))
    panel = [mine[0], other]
    for piece in mine[1:]:
        panel += [piece, lax.ppermute(piece, "row", swap)]
    rows, panel = lax.optimization_barrier((rows, panel))
    rows = lax.cond(leads, lambda x: x, exchange, rows)
    gram = jnp.sum(rows[:, own:].astype(f32), axis=0)
    chunk = RANK // n_peer
    gram = sum(along_y(gram[:chunk] + gram[chunk:2 * chunk] + gram[2 * chunk:3 * chunk]))
    parts, panel, rates = tile_pass(
        True, users, items, ratings[0, 0], rows, panel, own, tile_counts[0], gram
    )
    residual, shifted, sent = start_update(exchange(parts), prior_factors)
    direction = residual
    factors = prior_factors
    for iteration in range(ITERS):
        last = iteration == ITERS - 1
        rows = exchange(sent)
        parts = exchange(tile_pass(False, users, items, rates, rows, panel, own))
        out = update(last, parts, shifted, factors, residual, direction)
        if last:
            return tuple(out)
        factors, residual, direction, sent = out


def solution(mesh):
    placed = (
        P(("row", "col"), None),
        P(("row", "col"), None),
        P("row", "col", None),
        P("row", "col", None),
        P("row", "col"),
        P("row", "col", None, None, None),
    )
    return jax.shard_map(
        body,
        mesh=mesh,
        in_specs=placed,
        out_specs=(P(("row", "col"), None), P(("row", "col"), None)),
        check_vma=False,
    )
```

time: 231 us -> 214 us (0.926)
  the two profiles are of different devices: /device:TPU:24 before, /device:TPU:1 now
where the time goes in v3:
time: 214 us; the launch traced here: 213 us
  blocking collectives  142 us (66%)
  starting transfers between devices  26.9 us (13%)
  Pallas kernels  24.7 us (12%)
  waiting for transfers between devices  13.9 us (6%)
  local copies, waits for them, and re-layouts  4.29 us (2%)
    all_to_all x8, blocking collectives, exchange(): return lax.all_to_all(blocks, 'col', 0, 0, tiled=True)  142 us
    pallas_call x4, Pallas kernels, tile_pass(): pl.pallas_call(functools.partial(tile_kernel, first, n_peer, own, pieces)...  22.1 us
    ppermute x3, starting transfers between devices, body(): panel += [piece, lax.ppermute(piece, 'row', swap)]  18 us
    ppermute x6, waiting for transfers between devices, along_y(): lax.ppermute(x, 'row', [(r, (r + 2 * k) % n_row) for r in range(n_row)])  12.5 us
    ppermute x6, starting transfers between devices, along_y(): lax.ppermute(x, 'row', [(r, (r + 2 * k) % n_row) for r in range(n_row)])  5.54 us
  transfers between devices with their start and end apart: 10, of which 7 were waited for; matrix products, arithmetic and copies ran while one was open for 0% of the time, Pallas kernels for 0%

profile of v3, /device:TPU:1, one launch (start us, length us, event | category | flops | bytes accessed | tf_op | source)
XLA Modules:
  0.0 213.1 jit_solution(3754442830107533208)
XLA Ops:
  0.6 0.0 copy-start.6
  0.6 0.0 copy-start.5
  0.7 3.3 %collective-permute-start = (bf16[1024,128]{1,0:T(8,128)(2,1)}, bf16[1024,128]{1,0:T(8,128)(2,1)S(1)}, u32[]{:S(2)}, u32[]{:S(2)}) collective-permute-start(bf16[1024,128]{1,0:T(8,128)(2,1)} %rest_2_), channel_id=1, source_target_pairs={{0,32},{32,0},{64,96},{96,64},{128,160},{160,128},{192,224},{224,1... | collective-permute-start | bytes 786440 | tf_op jit(solution)/shard_map/ppermute | solution.py:327
  4.0 1.2 collective-permute-start.2
  5.2 0.4 collective-permute-start.1
  5.6 2.3 %collective-permute-start.3 = (bf16[1024,128]{1,0:T(8,128)(2,1)}, bf16[1024,128]{1,0:T(8,128)(2,1)S(1)}, u32[]{:S(2)}, u32[]{:S(2)}) collective-permute-start(bf16[1024,128]{1,0:T(8,128)(2,1)} %rest_2_), channel_id=1, source_target_pairs={{0,192},{32,224},{64,0},{96,32},{128,64},{160,96},{192,128},{224,1... | collective-permute-start | bytes 786440 | tf_op jit(solution)/shard_map/ppermute | solution.py:307
  7.9 0.0 collective-permute-done.other_ref.rest_3_
  7.9 1.0 copy-done.1
  8.8 0.8 copy-done.3
  9.6 0.4 prepare.1
  10.0 3.6 %collective-permute-done.2.rest_6_ = bf16[1024,128]{1,0:T(8,128)(2,1)S(1)} collective-permute-done((bf16[1024,128]{1,0:T(8,128)(2,1)}, bf16[1024,128]{1,0:T(8,128)(2,1)S(1)}, u32[]{:S(2)}, u32[]{:S(2)}) %collective-permute-start.2) | collective-permute-done | bytes 262176 | tf_op jit(solution)/shard_map/ppermute | solution.py:307
  13.6 6.0 %collective-permute-done.1.rest_4_ = bf16[1024,128]{1,0:T(8,128)(2,1)S(1)} collective-permute-done((bf16[1024,128]{1,0:T(8,128)(2,1)}, bf16[1024,128]{1,0:T(8,128)(2,1)S(1)}, u32[]{:S(2)}, u32[]{:S(2)}) %collective-permute-start.1) | collective-permute-done | bytes 262176 | tf_op jit(solution)/shard_map/ppermute | solution.py:307
  19.6 0.0 collective-permute-done.3.rest_8_
  19.6 17.5 %collective-permute-start.4 = (bf16[1024,128]{1,0:T(8,128)(2,1)S(1)}, bf16[1024,128]{1,0:T(8,128)(2,1)S(1)}, u32[]{:S(2)}, u32[]{:S(2)}) collective-permute-start(bf16[1024,128]{1,0:T(8,128)(2,1)S(1)} %collective-permute-done.1.rest_4_), channel_id=1, source_target_pairs={{0,32},{32,0},{64,96},{96,64},{128,160},{160,128},{192,224},{224,1... | collective-permute-start | bytes 786440 | tf_op jit(solution)/shard_map/ppermute | solution.py:336
  37.1 0.1 collective-permute-start.5
  37.2 0.4 collective-permute-start.6
  37.6 0.7 collective-permute-done.4.rest_5_
  38.3 0.4 collective-permute-done.5.rest_7_
  38.6 0.4 collective-permute-done.6.rest_9_
  39.0 18.0 %conditional.3 = (bf16[32,80,128]{2,1,0:T(8,128)(2,1)S(1)}) conditional(s32[]{:T(128)} %convert_element_type.11, bf16[32,80,128]{2,1,0:T(8,128)(2,1)S(1)} %get-tuple-element.68, bf16[32,80,128]{2,1,0:T(8,128)(2,1)S(1)} %get-tuple-element.68), branch_computations={%region_2.3_spmd, %region_3.4_spmd} | conditional | bytes 2621448 | solution.py:338
  39.1 18.0 %all_to_all.44 = bf16[32,80,128]{2,1,0:T(8,128)(2,1)S(1)} all-to-all(bf16[32,80,128]{2,1,0:T(8,128)(2,1)S(1)} %copy.14), channel_id=1, replica_groups=mesh['row'=8,'col'=32] {'col'}, dimensions={0} | all-to-all | bytes 1310720 | tf_op jit(solution)/shard_map/cond/branch_0_fun/all_to_all | solution.py:301
  57.1 0.1 collective-permute-start.8
  57.2 1.6 collective-permute-start.9
  58.8 0.0 collective-permute-start.7
  58.8 0.0 copy-done.6
  59.4 1.7 collective-permute-done.8
  61.1 0.0 collective-permute-done.9
  61.1 1.3 collective-permute-done.7
  62.4 0.0 copy-done.5
  62.4 0.0 copy-done.2
  62.4 0.0 copy-start.4
  62.4 9.9 %tile_start.1 = (s16[32,80,128]{2,1,0:T(8,128)(2,1)S(1)}, bf16[8192,128]{1,0:T(8,128)(2,1)S(1)}, bf16[40,256,256]{2,1,0:T(8,128)(2,1)}) custom-call(s32[40]{0:T(128)S(1)} %bitcast.17, s32[40]{0:T(128)S(1)} %fusion.items_ref, s32[40,256,256]{2,1,0:T(8,128)} %bitcast.21, bf16[32,80,128]{2,1,0:T(8,128)(2,1)S(1)} %get-tuple-element.69.rows_ref, ...), custom_call_target="tpu_custom_call" | custom-call | tf_op jit(solution)/shard_map/tile_start/pallas_call | solution.py:157
  72.3 19.6 %all_to_all.45.parts_ref = s16[32,80,128]{2,1,0:T(8,128)(2,1)S(1)} all-to-all(s16[32,80,128]{2,1,0:T(8,128)(2,1)S(1)} %get-tuple-element.55), channel_id=1, replica_groups=mesh['row'=8,'col'=32] {'col'}, dimensions={0} | all-to-all | bytes 1310720 | tf_op jit(solution)/shard_map/all_to_all | solution.py:301
  92.0 0.0 copy-done.4
  92.0 0.4 start_update.1
  92.4 18.5 %all_to_all.46.rows_ref = bf16[32,64,128]{2,1,0:T(8,128)(2,1)S(1)} all-to-all(bf16[32,64,128]{2,1,0:T(8,128)(2,1)S(1)} %get-tuple-element.56), channel_id=1, replica_groups=mesh['row'=8,'col'=32] {'col'}, dimensions={0} | all-to-all | bytes 1048576 | tf_op jit(solution)/shard_map/all_to_all | solution.py:301
  110.9 2.5 %copy-done = bf16[40,256,256]{2,1,0:T(8,128)(2,1)S(1)} copy-done((bf16[40,256,256]{2,1,0:T(8,128)(2,1)S(1)}, bf16[40,256,256]{2,1,0:T(8,128)(2,1)}, u32[]{:S(2)}) %copy-start) | copy-done | bytes 5242904
  113.4 4.1 %tile_pass.3 = s16[32,72,128]{2,1,0:T(8,128)(2,1)S(1)} custom-call(s32[40]{0:T(128)S(1)} %bitcast.18, s32[40]{0:T(128)S(1)} %fusion.items_ref, bf16[40,256,256]{2,1,0:T(8,128)(2,1)S(1)} %copy-done, bf16[32,64,128]{2,1,0:T(8,128)(2,1)S(1)} %all_to_all.46.rows_ref, bf16[8192,128]{1,0:T(8,128)(2,1)S(1)} %get-tuple-element.57.rest_0_), custom_call_target="tpu_custom_call" | custom-call | tf_op jit(solution)/shard_map/tile_pass/pallas_call | solution.py:157
  117.5 17.3 %all_to_all.47.parts_ref = s16[32,72,128]{2,1,0:T(8,128)(2,1)S(1)} all-to-all(s16[32,72,128]{2,1,0:T(8,128)(2,1)S(1)} %tile_pass.3), channel_id=1, replica_groups=mesh['row'=8,'col'=32] {'col'}, dimensions={0} | all-to-all | bytes 1179648 | tf_op jit(solution)/shard_map/all_to_all | solution.py:301
  134.8 0.5 update.2
  135.2 17.3 %all_to_all.48.rows_ref = bf16[32,64,128]{2,1,0:T(8,128)(2,1)S(1)} all-to-all(bf16[32,64,128]{2,1,0:T(8,128)(2,1)S(1)} %get-tuple-element.60), channel_id=1, replica_groups=mesh['row'=8,'col'=32] {'col'}, dimensions={0} | all-to-all | bytes 1048576 | tf_op jit(solution)/shard_map/all_to_all | solution.py:301
  152.6 4.1 %tile_pass.4 = s16[32,72,128]{2,1,0:T(8,128)(2,1)S(1)} custom-call(s32[40]{0:T(128)S(1)} %bitcast.19, s32[40]{0:T(128)S(1)} %fusion.items_ref, bf16[40,256,256]{2,1,0:T(8,128)(2,1)S(1)} %copy-done, bf16[32,64,128]{2,1,0:T(8,128)(2,1)S(1)} %all_to_all.48.rows_ref, bf16[8192,128]{1,0:T(8,128)(2,1)S(1)} %get-tuple-element.57.rest_0_), custom_call_target="tpu_custom_call" | custom-call | tf_op jit(solution)/shard_map/tile_pass/pallas_call | solution.py:157
  156.6 17.1 %all_to_all.49.parts_ref = s16[32,72,128]{2,1,0:T(8,128)(2,1)S(1)} all-to-all(s16[32,72,128]{2,1,0:T(8,128)(2,1)S(1)} %tile_pass.4), channel_id=1, replica_groups=mesh['row'=8,'col'=32] {'col'}, dimensions={0} | all-to-all | bytes 1179648 | tf_op jit(solution)/shard_map/all_to_all | solution.py:301
  173.8 0.5 update.3
  174.2 16.7 %all_to_all.50.rows_ref = bf16[32,64,128]{2,1,0:T(8,128)(2,1)S(1)} all-to-all(bf16[32,64,128]{2,1,0:T(8,128)(2,1)S(1)} %get-tuple-element.64), channel_id=1, replica_groups=mesh['row'=8,'col'=32] {'col'}, dimensions={0} | all-to-all | bytes 1048576 | tf_op jit(solution)/shard_map/all_to_all | solution.py:301
  190.9 4.1 %tile_pass.5 = s16[32,72,128]{2,1,0:T(8,128)(2,1)S(1)} custom-call(s32[40]{0:T(128)S(1)} %bitcast.20, s32[40]{0:T(128)S(1)} %fusion.items_ref, bf16[40,256,256]{2,1,0:T(8,128)(2,1)S(1)} %copy-done, bf16[32,64,128]{2,1,0:T(8,128)(2,1)S(1)} %all_to_all.50.rows_ref, bf16[8192,128]{1,0:T(8,128)(2,1)S(1)} %get-tuple-element.57.rest_0_), custom_call_target="tpu_custom_call" | custom-call | tf_op jit(solution)/shard_map/tile_pass/pallas_call | solution.py:157
  195.0 17.1 %all_to_all.51.parts_ref = s16[32,72,128]{2,1,0:T(8,128)(2,1)S(1)} all-to-all(s16[32,72,128]{2,1,0:T(8,128)(2,1)S(1)} %tile_pass.5), channel_id=1, replica_groups=mesh['row'=8,'col'=32] {'col'}, dimensions={0} | all-to-all | bytes 1179648 | tf_op jit(solution)/shard_map/all_to_all | solution.py:301
  212.1 1.0 update_last.1
  (10 shorter events, 0.1 us)
Async XLA Ops:
  0.6 58.1 %copy-start.6 = (s32[1,1,40]{2,1,0:T(1,128)S(1)}, s32[1,1,40]{2,1,0:T(1,128)}, u32[]{:S(2)}) copy-start(s32[1,1,40]{2,1,0:T(1,128)} %param.13) | copy-start | bytes 484
  0.6 61.8 %copy-start.5 = (s32[1,1,40]{2,1,0:T(1,128)S(1)}, s32[1,1,40]{2,1,0:T(1,128)}, u32[]{:S(2)}) copy-start(s32[1,1,40]{2,1,0:T(1,128)} %param.12) | copy-start | bytes 484
  0.7 7.2 %collective-permute-start = (bf16[1024,128]{1,0:T(8,128)(2,1)}, bf16[1024,128]{1,0:T(8,128)(2,1)S(1)}, u32[]{:S(2)}, u32[]{:S(2)}) collective-permute-start(bf16[1024,128]{1,0:T(8,128)(2,1)} %rest_2_), channel_id=1, source_target_pairs={{0,32},{32,0},{64,96},{96,64},{128,160},{160,128},{192,224},{224,1... | collective-permute-start | bytes 786440 | tf_op jit(solution)/shard_map/ppermute | solution.py:327
  4.0 9.6 %collective-permute-start.2 = (bf16[1024,128]{1,0:T(8,128)(2,1)}, bf16[1024,128]{1,0:T(8,128)(2,1)S(1)}, u32[]{:S(2)}, u32[]{:S(2)}) collective-permute-start(bf16[1024,128]{1,0:T(8,128)(2,1)} %rest_2_), channel_id=1, source_target_pairs={{0,128},{32,160},{64,192},{96,224},{128,0},{160,32},{192,64},{224,... | collective-permute-start | bytes 786440 | tf_op jit(solution)/shard_map/ppermute | solution.py:307
  5.2 14.4 %collective-permute-start.1 = (bf16[1024,128]{1,0:T(8,128)(2,1)}, bf16[1024,128]{1,0:T(8,128)(2,1)S(1)}, u32[]{:S(2)}, u32[]{:S(2)}) collective-permute-start(bf16[1024,128]{1,0:T(8,128)(2,1)} %rest_2_), channel_id=1, source_target_pairs={{0,64},{32,96},{64,128},{96,160},{128,192},{160,224},{192,0},{224,... | collective-permute-start | bytes 786440 | tf_op jit(solution)/shard_map/ppermute | solution.py:307
  5.6 14.0 %collective-permute-start.3 = (bf16[1024,128]{1,0:T(8,128)(2,1)}, bf16[1024,128]{1,0:T(8,128)(2,1)S(1)}, u32[]{:S(2)}, u32[]{:S(2)}) collective-permute-start(bf16[1024,128]{1,0:T(8,128)(2,1)} %rest_2_), channel_id=1, source_target_pairs={{0,192},{32,224},{64,0},{96,32},{128,64},{160,96},{192,128},{224,1... | collective-permute-start | bytes 786440 | tf_op jit(solution)/shard_map/ppermute | solution.py:307
  7.9 1.0 copy-start.1
  8.8 0.8 copy-start.3
  9.6 52.8 %copy-start.2 = (bf16[1024,128]{1,0:T(8,128)(2,1)S(1)}, bf16[1024,128]{1,0:T(8,128)(2,1)}, u32[]{:S(2)}) copy-start(bf16[1024,128]{1,0:T(8,128)(2,1)} %rest_2_) | copy-start | bytes 786436
  19.6 18.7 %collective-permute-start.4 = (bf16[1024,128]{1,0:T(8,128)(2,1)S(1)}, bf16[1024,128]{1,0:T(8,128)(2,1)S(1)}, u32[]{:S(2)}, u32[]{:S(2)}) collective-permute-start(bf16[1024,128]{1,0:T(8,128)(2,1)S(1)} %collective-permute-done.1.rest_4_), channel_id=1, source_target_pairs={{0,32},{32,0},{64,96},{96,64},{128,160},{160,128},{192,224},{224,1... | collective-permute-start | bytes 786440 | tf_op jit(solution)/shard_map/ppermute | solution.py:336
  37.1 1.5 collective-permute-start.5
  37.2 1.8 collective-permute-start.6
  57.1 4.0 %collective-permute-start.8 = (f32[4,128]{1,0:T(4,128)S(1)}, f32[4,128]{1,0:T(4,128)S(1)}, u32[]{:S(2)}, u32[]{:S(2)}) collective-permute-start(f32[4,128]{1,0:T(4,128)S(1)} %slice_add_fusion), channel_id=1, source_target_pairs={{0,128},{32,160},{64,192},{96,224},{128,0},{160,32},{192,64},{224,... | collective-permute-start | bytes 6152 | tf_op jit(solution)/shard_map/ppermute | solution.py:307
  57.2 3.9 %collective-permute-start.9 = (f32[4,128]{1,0:T(4,128)S(1)}, f32[4,128]{1,0:T(4,128)S(1)}, u32[]{:S(2)}, u32[]{:S(2)}) collective-permute-start(f32[4,128]{1,0:T(4,128)S(1)} %slice_add_fusion), channel_id=1, source_target_pairs={{0,192},{32,224},{64,0},{96,32},{128,64},{160,96},{192,128},{224,1... | collective-permute-start | bytes 6152 | tf_op jit(solution)/shard_map/ppermute | solution.py:307
  58.8 3.6 %collective-permute-start.7 = (f32[4,128]{1,0:T(4,128)S(1)}, f32[4,128]{1,0:T(4,128)S(1)}, u32[]{:S(2)}, u32[]{:S(2)}) collective-permute-start(f32[4,128]{1,0:T(4,128)S(1)} %slice_add_fusion), channel_id=1, source_target_pairs={{0,64},{32,96},{64,128},{96,160},{128,192},{160,224},{192,0},{224,... | collective-permute-start | bytes 6152 | tf_op jit(solution)/shard_map/ppermute | solution.py:307
  62.4 29.6 %copy-start.4 = (f32[64,128]{1,0:T(8,128)S(1)}, f32[64,128]{1,0:T(8,128)}, u32[]{:S(2)}) copy-start(f32[64,128]{1,0:T(8,128)} %factors_ref.1) | copy-start | bytes 98308
  110.9 2.5 %copy-start = (bf16[40,256,256]{2,1,0:T(8,128)(2,1)S(1)}, bf16[40,256,256]{2,1,0:T(8,128)(2,1)}, u32[]{:S(2)}) copy-start(bf16[40,256,256]{2,1,0:T(8,128)(2,1)} %get-tuple-element.54.rates) | copy-start | bytes 15728644

commit v4 on v3

--- a/solution.py
+++ b/solution.py
@@ -21,7 +21,7 @@
 bf16 = jnp.bfloat16
 f32 = jnp.float32
 VMEM_LIMIT = 24 * 1024 * 1024
-START_LIMIT = 46 * 1024 * 1024
+START_LIMIT = 40 * 1024 * 1024
 
 
 def params(limit=VMEM_LIMIT):

time: 214 us -> 209 us (0.977)
  local copies, waits for them, and re-layouts: 4.29 us -> 1.8 us
  Pallas kernels: 24.7 us -> 22.4 us
    unnamed x14 -> x12, local copies, waits for them, and re-layouts: 4.24 us -> 1.76 us
    pallas_call x4, Pallas kernels: 22.1 us -> 19.8 us  [tile_pass(): pl.pallas_call(functools.partial(tile_kernel, first, n_peer, own, pieces)...]
where the time goes in v4:
time: 209 us; the launch traced here: 208 us
  blocking collectives  142 us (68%)
  starting transfers between devices  26.9 us (13%)
  Pallas kernels  22.4 us (11%)
  waiting for transfers between devices  13.9 us (7%)
    all_to_all x8, blocking collectives, exchange(): return lax.all_to_all(blocks, 'col', 0, 0, tiled=True)  142 us
    pallas_call x4, Pallas kernels, tile_pass(): pl.pallas_call(functools.partial(tile_kernel, first, n_peer, own, pieces)...  19.8 us
    ppermute x3, starting transfers between devices, body(): panel += [piece, lax.ppermute(piece, 'row', swap)]  18 us
    ppermute x6, waiting for transfers between devices, along_y(): lax.ppermute(x, 'row', [(r, (r + 2 * k) % n_row) for r in range(n_row)])  12.5 us
    ppermute x6, starting transfers between devices, along_y(): lax.ppermute(x, 'row', [(r, (r + 2 * k) % n_row) for r in range(n_row)])  5.54 us
  transfers between devices with their start and end apart: 10, of which 7 were waited for; matrix products, arithmetic and copies ran while one was open for 0% of the time, Pallas kernels for 0%

profile of v4, /device:TPU:1, one launch (start us, length us, event | category | flops | bytes accessed | tf_op | source)
XLA Modules:
  0.0 208.3 jit_solution(15045414318147587308)
XLA Ops:
  0.6 0.0 copy-start.5
  0.6 0.0 copy-start.4
  0.7 3.3 %collective-permute-start = (bf16[1024,128]{1,0:T(8,128)(2,1)}, bf16[1024,128]{1,0:T(8,128)(2,1)S(1)}, u32[]{:S(2)}, u32[]{:S(2)}) collective-permute-start(bf16[1024,128]{1,0:T(8,128)(2,1)} %rest_2_), channel_id=1, source_target_pairs={{0,32},{32,0},{64,96},{96,64},{128,160},{160,128},{192,224},{224,1... | collective-permute-start | bytes 786440 | tf_op jit(solution)/shard_map/ppermute | solution.py:327
  4.0 1.2 collective-permute-start.2
  5.2 0.4 collective-permute-start.1
  5.6 2.3 %collective-permute-start.3 = (bf16[1024,128]{1,0:T(8,128)(2,1)}, bf16[1024,128]{1,0:T(8,128)(2,1)S(1)}, u32[]{:S(2)}, u32[]{:S(2)}) collective-permute-start(bf16[1024,128]{1,0:T(8,128)(2,1)} %rest_2_), channel_id=1, source_target_pairs={{0,192},{32,224},{64,0},{96,32},{128,64},{160,96},{192,128},{224,1... | collective-permute-start | bytes 786440 | tf_op jit(solution)/shard_map/ppermute | solution.py:307
  7.9 0.0 collective-permute-done.other_ref.rest_3_
  7.9 0.0 copy-start
  7.9 1.0 copy-done
  8.8 0.8 copy-done.2
  9.6 0.4 prepare.1
  10.0 3.6 %collective-permute-done.2.rest_6_ = bf16[1024,128]{1,0:T(8,128)(2,1)S(1)} collective-permute-done((bf16[1024,128]{1,0:T(8,128)(2,1)}, bf16[1024,128]{1,0:T(8,128)(2,1)S(1)}, u32[]{:S(2)}, u32[]{:S(2)}) %collective-permute-start.2) | collective-permute-done | bytes 262176 | tf_op jit(solution)/shard_map/ppermute | solution.py:307
  13.6 6.0 %collective-permute-done.1.rest_4_ = bf16[1024,128]{1,0:T(8,128)(2,1)S(1)} collective-permute-done((bf16[1024,128]{1,0:T(8,128)(2,1)}, bf16[1024,128]{1,0:T(8,128)(2,1)S(1)}, u32[]{:S(2)}, u32[]{:S(2)}) %collective-permute-start.1) | collective-permute-done | bytes 262176 | tf_op jit(solution)/shard_map/ppermute | solution.py:307
  19.6 0.0 collective-permute-done.3.rest_8_
  19.6 17.5 %collective-permute-start.4 = (bf16[1024,128]{1,0:T(8,128)(2,1)S(1)}, bf16[1024,128]{1,0:T(8,128)(2,1)S(1)}, u32[]{:S(2)}, u32[]{:S(2)}) collective-permute-start(bf16[1024,128]{1,0:T(8,128)(2,1)S(1)} %collective-permute-done.1.rest_4_), channel_id=1, source_target_pairs={{0,32},{32,0},{64,96},{96,64},{128,160},{160,128},{192,224},{224,1... | collective-permute-start | bytes 786440 | tf_op jit(solution)/shard_map/ppermute | solution.py:336
  37.1 0.1 collective-permute-start.5
  37.2 0.4 collective-permute-start.6
  37.6 0.7 collective-permute-done.4.rest_5_
  38.3 0.4 collective-permute-done.5.rest_7_
  38.6 0.4 collective-permute-done.6.rest_9_
  39.0 18.0 %conditional.3 = (bf16[32,80,128]{2,1,0:T(8,128)(2,1)S(1)}) conditional(s32[]{:T(128)} %convert_element_type.11, bf16[32,80,128]{2,1,0:T(8,128)(2,1)S(1)} %get-tuple-element.68, bf16[32,80,128]{2,1,0:T(8,128)(2,1)S(1)} %get-tuple-element.68), branch_computations={%region_2.3_spmd, %region_3.4_spmd} | conditional | bytes 2621448 | solution.py:338
  39.1 18.0 %all_to_all.44 = bf16[32,80,128]{2,1,0:T(8,128)(2,1)S(1)} all-to-all(bf16[32,80,128]{2,1,0:T(8,128)(2,1)S(1)} %copy.14), channel_id=1, replica_groups=mesh['row'=8,'col'=32] {'col'}, dimensions={0} | all-to-all | bytes 1310720 | tf_op jit(solution)/shard_map/cond/branch_0_fun/all_to_all | solution.py:301
  57.1 0.1 collective-permute-start.8
  57.2 1.6 collective-permute-start.9
  58.8 0.0 collective-permute-start.7
  58.8 0.0 copy-done.5
  59.4 1.7 collective-permute-done.8
  61.1 0.0 collective-permute-done.9
  61.1 1.3 collective-permute-done.7
  62.4 0.0 copy-done.4
  62.4 0.0 copy-done.1
  62.4 0.0 copy-start.3
  62.4 7.8 %tile_start.1 = (s16[32,80,128]{2,1,0:T(8,128)(2,1)S(1)}, bf16[8192,128]{1,0:T(8,128)(2,1)S(1)}, bf16[40,256,256]{2,1,0:T(8,128)(2,1)S(1)}) custom-call(s32[40]{0:T(128)S(1)} %bitcast.17, s32[40]{0:T(128)S(1)} %fusion.items_ref, s32[40,256,256]{2,1,0:T(8,128)} %bitcast.21, bf16[32,80,128]{2,1,0:T(8,128)(2,1)S(1)} %get-tuple-element.69.rows_ref, ...), custom_call_target="tpu_custom_call" | custom-call | tf_op jit(solution)/shard_map/tile_start/pallas_call | solution.py:157
  70.2 19.6 %all_to_all.45.parts_ref = s16[32,80,128]{2,1,0:T(8,128)(2,1)S(1)} all-to-all(s16[32,80,128]{2,1,0:T(8,128)(2,1)S(1)} %get-tuple-element.55), channel_id=1, replica_groups=mesh['row'=8,'col'=32] {'col'}, dimensions={0} | all-to-all | bytes 1310720 | tf_op jit(solution)/shard_map/all_to_all | solution.py:301
  89.9 0.0 copy-done.3
  89.9 0.4 start_update.1
  90.2 18.5 %all_to_all.46.rows_ref = bf16[32,64,128]{2,1,0:T(8,128)(2,1)S(1)} all-to-all(bf16[32,64,128]{2,1,0:T(8,128)(2,1)S(1)} %get-tuple-element.56), channel_id=1, replica_groups=mesh['row'=8,'col'=32] {'col'}, dimensions={0} | all-to-all | bytes 1048576 | tf_op jit(solution)/shard_map/all_to_all | solution.py:301
  108.8 4.0 %tile_pass.3 = s16[32,72,128]{2,1,0:T(8,128)(2,1)S(1)} custom-call(s32[40]{0:T(128)S(1)} %bitcast.18, s32[40]{0:T(128)S(1)} %fusion.items_ref, bf16[40,256,256]{2,1,0:T(8,128)(2,1)S(1)} %get-tuple-element.54.rates, bf16[32,64,128]{2,1,0:T(8,128)(2,1)S(1)} %all_to_all.46.rows_ref, bf16[8192,128]{1,0:T(8,128)(2,1)S(1)} %get-tuple-element.57.rest_0_), custom_call_target="tpu_custom_call" | custom-call | tf_op jit(solution)/shard_map/tile_pass/pallas_call | solution.py:157
  112.8 17.3 %all_to_all.47.parts_ref = s16[32,72,128]{2,1,0:T(8,128)(2,1)S(1)} all-to-all(s16[32,72,128]{2,1,0:T(8,128)(2,1)S(1)} %tile_pass.3), channel_id=1, replica_groups=mesh['row'=8,'col'=32] {'col'}, dimensions={0} | all-to-all | bytes 1179648 | tf_op jit(solution)/shard_map/all_to_all | solution.py:301
  130.1 0.5 update.2
  130.5 17.3 %all_to_all.48.rows_ref = bf16[32,64,128]{2,1,0:T(8,128)(2,1)S(1)} all-to-all(bf16[32,64,128]{2,1,0:T(8,128)(2,1)S(1)} %get-tuple-element.60), channel_id=1, replica_groups=mesh['row'=8,'col'=32] {'col'}, dimensions={0} | all-to-all | bytes 1048576 | tf_op jit(solution)/shard_map/all_to_all | solution.py:301
  147.8 4.0 %tile_pass.4 = s16[32,72,128]{2,1,0:T(8,128)(2,1)S(1)} custom-call(s32[40]{0:T(128)S(1)} %bitcast.19, s32[40]{0:T(128)S(1)} %fusion.items_ref, bf16[40,256,256]{2,1,0:T(8,128)(2,1)S(1)} %get-tuple-element.54.rates, bf16[32,64,128]{2,1,0:T(8,128)(2,1)S(1)} %all_to_all.48.rows_ref, bf16[8192,128]{1,0:T(8,128)(2,1)S(1)} %get-tuple-element.57.rest_0_), custom_call_target="tpu_custom_call" | custom-call | tf_op jit(solution)/shard_map/tile_pass/pallas_call | solution.py:157
  151.8 17.1 %all_to_all.49.parts_ref = s16[32,72,128]{2,1,0:T(8,128)(2,1)S(1)} all-to-all(s16[32,72,128]{2,1,0:T(8,128)(2,1)S(1)} %tile_pass.4), channel_id=1, replica_groups=mesh['row'=8,'col'=32] {'col'}, dimensions={0} | all-to-all | bytes 1179648 | tf_op jit(solution)/shard_map/all_to_all | solution.py:301
  169.0 0.5 update.3
  169.4 16.7 %all_to_all.50.rows_ref = bf16[32,64,128]{2,1,0:T(8,128)(2,1)S(1)} all-to-all(bf16[32,64,128]{2,1,0:T(8,128)(2,1)S(1)} %get-tuple-element.64), channel_id=1, replica_groups=mesh['row'=8,'col'=32] {'col'}, dimensions={0} | all-to-all | bytes 1048576 | tf_op jit(solution)/shard_map/all_to_all | solution.py:301
  186.1 4.0 %tile_pass.5 = s16[32,72,128]{2,1,0:T(8,128)(2,1)S(1)} custom-call(s32[40]{0:T(128)S(1)} %bitcast.20, s32[40]{0:T(128)S(1)} %fusion.items_ref, bf16[40,256,256]{2,1,0:T(8,128)(2,1)S(1)} %get-tuple-element.54.rates, bf16[32,64,128]{2,1,0:T(8,128)(2,1)S(1)} %all_to_all.50.rows_ref, bf16[8192,128]{1,0:T(8,128)(2,1)S(1)} %get-tuple-element.57.rest_0_), custom_call_target="tpu_custom_call" | custom-call | tf_op jit(solution)/shard_map/tile_pass/pallas_call | solution.py:157
  190.2 17.2 %all_to_all.51.parts_ref = s16[32,72,128]{2,1,0:T(8,128)(2,1)S(1)} all-to-all(s16[32,72,128]{2,1,0:T(8,128)(2,1)S(1)} %tile_pass.5), channel_id=1, replica_groups=mesh['row'=8,'col'=32] {'col'}, dimensions={0} | all-to-all | bytes 1179648 | tf_op jit(solution)/shard_map/all_to_all | solution.py:301
  207.3 1.0 update_last.1
  (8 shorter events, 0.1 us)
Async XLA Ops:
  0.6 58.1 %copy-start.5 = (s32[1,1,40]{2,1,0:T(1,128)S(1)}, s32[1,1,40]{2,1,0:T(1,128)}, u32[]{:S(2)}) copy-start(s32[1,1,40]{2,1,0:T(1,128)} %param.13) | copy-start | bytes 484
  0.6 61.8 %copy-start.4 = (s32[1,1,40]{2,1,0:T(1,128)S(1)}, s32[1,1,40]{2,1,0:T(1,128)}, u32[]{:S(2)}) copy-start(s32[1,1,40]{2,1,0:T(1,128)} %param.12) | copy-start | bytes 484
  0.7 7.2 %collective-permute-start = (bf16[1024,128]{1,0:T(8,128)(2,1)}, bf16[1024,128]{1,0:T(8,128)(2,1)S(1)}, u32[]{:S(2)}, u32[]{:S(2)}) collective-permute-start(bf16[1024,128]{1,0:T(8,128)(2,1)} %rest_2_), channel_id=1, source_target_pairs={{0,32},{32,0},{64,96},{96,64},{128,160},{160,128},{192,224},{224,1... | collective-permute-start | bytes 786440 | tf_op jit(solution)/shard_map/ppermute | solution.py:327
  4.0 9.6 %collective-permute-start.2 = (bf16[1024,128]{1,0:T(8,128)(2,1)}, bf16[1024,128]{1,0:T(8,128)(2,1)S(1)}, u32[]{:S(2)}, u32[]{:S(2)}) collective-permute-start(bf16[1024,128]{1,0:T(8,128)(2,1)} %rest_2_), channel_id=1, source_target_pairs={{0,128},{32,160},{64,192},{96,224},{128,0},{160,32},{192,64},{224,... | collective-permute-start | bytes 786440 | tf_op jit(solution)/shard_map/ppermute | solution.py:307
  5.2 14.4 %collective-permute-start.1 = (bf16[1024,128]{1,0:T(8,128)(2,1)}, bf16[1024,128]{1,0:T(8,128)(2,1)S(1)}, u32[]{:S(2)}, u32[]{:S(2)}) collective-permute-start(bf16[1024,128]{1,0:T(8,128)(2,1)} %rest_2_), channel_id=1, source_target_pairs={{0,64},{32,96},{64,128},{96,160},{128,192},{160,224},{192,0},{224,... | collective-permute-start | bytes 786440 | tf_op jit(solution)/shard_map/ppermute | solution.py:307
  5.6 14.0 %collective-permute-start.3 = (bf16[1024,128]{1,0:T(8,128)(2,1)}, bf16[1024,128]{1,0:T(8,128)(2,1)S(1)}, u32[]{:S(2)}, u32[]{:S(2)}) collective-permute-start(bf16[1024,128]{1,0:T(8,128)(2,1)} %rest_2_), channel_id=1, source_target_pairs={{0,192},{32,224},{64,0},{96,32},{128,64},{160,96},{192,128},{224,1... | collective-permute-start | bytes 786440 | tf_op jit(solution)/shard_map/ppermute | solution.py:307
  7.9 1.0 copy-start
  8.8 0.8 copy-start.2
  9.6 52.8 %copy-start.1 = (bf16[1024,128]{1,0:T(8,128)(2,1)S(1)}, bf16[1024,128]{1,0:T(8,128)(2,1)}, u32[]{:S(2)}) copy-start(bf16[1024,128]{1,0:T(8,128)(2,1)} %rest_2_) | copy-start | bytes 786436
  19.6 18.7 %collective-permute-start.4 = (bf16[1024,128]{1,0:T(8,128)(2,1)S(1)}, bf16[1024,128]{1,0:T(8,128)(2,1)S(1)}, u32[]{:S(2)}, u32[]{:S(2)}) collective-permute-start(bf16[1024,128]{1,0:T(8,128)(2,1)S(1)} %collective-permute-done.1.rest_4_), channel_id=1, source_target_pairs={{0,32},{32,0},{64,96},{96,64},{128,160},{160,128},{192,224},{224,1... | collective-permute-start | bytes 786440 | tf_op jit(solution)/shard_map/ppermute | solution.py:336
  37.1 1.5 collective-permute-start.5
  37.2 1.8 collective-permute-start.6
  57.1 4.0 %collective-permute-start.8 = (f32[4,128]{1,0:T(4,128)S(1)}, f32[4,128]{1,0:T(4,128)S(1)}, u32[]{:S(2)}, u32[]{:S(2)}) collective-permute-start(f32[4,128]{1,0:T(4,128)S(1)} %slice_add_fusion), channel_id=1, source_target_pairs={{0,128},{32,160},{64,192},{96,224},{128,0},{160,32},{192,64},{224,... | collective-permute-start | bytes 6152 | tf_op jit(solution)/shard_map/ppermute | solution.py:307
  57.2 3.9 %collective-permute-start.9 = (f32[4,128]{1,0:T(4,128)S(1)}, f32[4,128]{1,0:T(4,128)S(1)}, u32[]{:S(2)}, u32[]{:S(2)}) collective-permute-start(f32[4,128]{1,0:T(4,128)S(1)} %slice_add_fusion), channel_id=1, source_target_pairs={{0,192},{32,224},{64,0},{96,32},{128,64},{160,96},{192,128},{224,1... | collective-permute-start | bytes 6152 | tf_op jit(solution)/shard_map/ppermute | solution.py:307
  58.8 3.6 %collective-permute-start.7 = (f32[4,128]{1,0:T(4,128)S(1)}, f32[4,128]{1,0:T(4,128)S(1)}, u32[]{:S(2)}, u32[]{:S(2)}) collective-permute-start(f32[4,128]{1,0:T(4,128)S(1)} %slice_add_fusion), channel_id=1, source_target_pairs={{0,64},{32,96},{64,128},{96,160},{128,192},{160,224},{192,0},{224,... | collective-permute-start | bytes 6152 | tf_op jit(solution)/shard_map/ppermute | solution.py:307
  62.4 27.4 %copy-start.3 = (f32[64,128]{1,0:T(8,128)S(1)}, f32[64,128]{1,0:T(8,128)}, u32[]{:S(2)}) copy-start(f32[64,128]{1,0:T(8,128)} %factors_ref.1) | copy-start | bytes 98308

commit v5 on v4

--- a/solution.py
+++ b/solution.py
@@ -50,9 +50,9 @@
 
 def tile_kernel(first, n_peer, own, pieces, users_ref, items_ref, rates, rows_ref, *rest):
     if first:
-        count_ref, gram_ref = rest[:2]
-        panel_hbm = rest[2:2 + pieces]
-        out_ref, panel, scaled_rates, total, panel_sems, ratings, rate_sems = rest[2 + pieces:]
+        count_ref = rest[0]
+        panel_hbm = rest[1:1 + pieces]
+        out_ref, panel, scaled_rates, total, panel_sems, ratings, rate_sems = rest[1 + pieces:]
         rates_hbm, rates = rates, ratings
     else:
         panel, out_ref, total = rest
@@ -116,21 +116,13 @@
     powers = jnp.concatenate([bound_power(total[p]) for p in range(n_peer)], axis=0)
     factors = power_of_two(-powers) * CODE_TOP
     extra = [jnp.zeros((lead - 1, RANK), jnp.int32)]
-    if first:
-        gram = gram_ref[...]
-        gram_power = bound_power(gram)
-        scaled = gram * (power_of_two(-gram_power) * CODE_TOP)
-        gram_high = whole(scaled)
-        gram_low = whole((scaled - gram_high.astype(f32)) * CODE_TOP)
-        extra = [gram_power.astype(jnp.int32), gram_high, gram_low,
-                 jnp.zeros((lead - 2 - 2 * gram.shape[0], RANK), jnp.int32)]
     for p in range(n_peer):
         out_ref[p, :own] = whole(total[p] * factors[p:p + 1]).astype(jnp.int16)
         lines = [powers[p:p + 1].astype(jnp.int32)] + extra
         out_ref[p, own:] = jnp.concatenate(lines, axis=0).astype(jnp.int16)
 
 
-def tile_pass(first, users, items, rates, rows, panel, own, count=None, gram=None):
+def tile_pass(first, users, items, rates, rows, panel, own, count=None):
     n_peer = rows.shape[0]
     vmem = pl.BlockSpec(memory_space=pltpu.VMEM)
     smem = pl.BlockSpec(memory_space=pltpu.SMEM)
@@ -149,8 +141,8 @@
         scratch.append(pltpu.VMEM(rates.shape, rates.dtype))
         scratch.append(pltpu.SemaphoreType.DMA((rates.shape[0] // 8,)))
         specs[2] = hbm
-        specs += [smem, vmem] + [hbm] * pieces
-        operands += [count, gram] + list(panel)
+        specs += [smem] + [hbm] * pieces
+        operands += [count] + list(panel)
     else:
         specs.append(vmem)
         operands.append(panel)
@@ -161,9 +153,41 @@
         out_shape=out_shape,
         scratch_shapes=scratch,
         compiler_params=params(START_LIMIT if first else VMEM_LIMIT),
+        cost_estimate=pl.CostEstimate(
+            flops=4 * rates.shape[0] * TILE * TILE * RANK,
+            bytes_accessed=rates.size * rates.dtype.itemsize,
+            transcendentals=0,
+        ),
         name="tile_start" if first else "tile_pass",
     )(*operands)
     return out if first else out[0]
+
+
+def insert_kernel(own, parts_ref, gram_ref, out_ref):
+    gram = gram_ref[...]
+    gram_power = bound_power(gram)
+    scaled = gram * (power_of_two(-gram_power) * CODE_TOP)
+    gram_high = whole(scaled)
+    gram_low = whole((scaled - gram_high.astype(f32)) * CODE_TOP)
+    lead = out_ref.shape[1] - own
+    lines = [gram_power.astype(jnp.int32), gram_high, gram_low,
+             jnp.zeros((lead - 2 - 2 * gram.shape[0], RANK), jnp.int32)]
+    for p in range(out_ref.shape[0]):
+        out_ref[p, :own] = parts_ref[p, :own]
+        power = parts_ref[p, own:].astype(jnp.int32)[:1]
+        out_ref[p, own:] = jnp.concatenate([power] + lines, axis=0).astype(jnp.int16)
+
+
+def insert(parts, gram, own):
+    vmem = pl.BlockSpec(memory_space=pltpu.VMEM)
+    return pl.pallas_call(
+        functools.partial(insert_kernel, own),
+        in_specs=[vmem] * 2,
+        out_specs=vmem,
+        out_shape=jax.ShapeDtypeStruct(parts.shape, parts.dtype),
+        compiler_params=params(),
+        name="insert",
+    )(parts, gram)
 
 
 def code_lines(parts_ref, own):
@@ -340,8 +364,9 @@
     chunk = RANK // n_peer
     gram = sum(along_y(gram[:chunk] + gram[chunk:2 * chunk] + gram[2 * chunk:3 * chunk]))
     parts, panel, rates = tile_pass(
-        True, users, items, ratings[0, 0], rows, panel, own, tile_counts[0], gram
-    )
+        True, users, items, ratings[0, 0], rows, panel, own, tile_counts[0]
+    )
+    parts = insert(parts, gram, own)
     residual, shifted, sent = start_update(exchange(parts), prior_factors)
     direction = residual
     factors = prior_factors

time: 209 us -> 209 us (level)
  waiting for transfers between devices: 13.9 us -> 9.86 us
  blocking collectives: 142 us -> 146 us
    all_to_all x8, blocking collectives: 142 us -> 146 us  [exchange(): return lax.all_to_all(blocks, 'col', 0, 0, tiled=True)]
    ppermute x6, waiting for transfers between devices: 12.5 us -> 9.81 us  [along_y(): lax.ppermute(x, 'row', [(r, (r + 2 * k) % n_row) for r in range(n_row)])]
  transfers between devices with their start and end apart: 10 -> 10, of which waited for: 7 -> 3; matrix products, arithmetic and copies ran while one was open for 0% -> 0% of each run, Pallas kernels for 0% -> 4%
where the time goes in v5:
time: 209 us
  blocking collectives  146 us (70%)
  starting transfers between devices  26.7 us (13%)
  Pallas kernels  22.2 us (11%)
  waiting for transfers between devices  9.86 us (5%)
    all_to_all x8, blocking collectives, exchange(): return lax.all_to_all(blocks, 'col', 0, 0, tiled=True)  146 us
    pallas_call x4, Pallas kernels, tile_pass(): pl.pallas_call(functools.partial(tile_kernel, first, n_peer, own, pieces)...  19.5 us
    ppermute x3, starting transfers between devices, body(): panel += [piece, lax.ppermute(piece, 'row', swap)]  17.8 us
    ppermute x6, waiting for transfers between devices, along_y(): lax.ppermute(x, 'row', [(r, (r + 2 * k) % n_row) for r in range(n_row)])  9.81 us
    ppermute x6, starting transfers between devices, along_y(): lax.ppermute(x, 'row', [(r, (r + 2 * k) % n_row) for r in range(n_row)])  5.52 us
  transfers between devices with their start and end apart: 10, of which 3 were waited for; matrix products, arithmetic and copies ran while one was open for 0% of the time, Pallas kernels for 4%

profile of v5, /device:TPU:1, one launch (start us, length us, event | category | flops | bytes accessed | tf_op | source)
XLA Modules:
  0.0 208.5 jit_solution(11601718339478771072)
XLA Ops:
  0.6 0.0 copy-start.4
  0.6 3.3 %collective-permute-start = (bf16[1024,128]{1,0:T(8,128)(2,1)}, bf16[1024,128]{1,0:T(8,128)(2,1)S(1)}, u32[]{:S(2)}, u32[]{:S(2)}) collective-permute-start(bf16[1024,128]{1,0:T(8,128)(2,1)} %rest_1_), channel_id=1, source_target_pairs={{0,32},{32,0},{64,96},{96,64},{128,160},{160,128},{192,224},{224,1... | collective-permute-start | bytes 786440 | tf_op jit(solution)/shard_map/ppermute | solution.py:351
  4.0 0.0 collective-permute-start.1
  4.0 2.2 %collective-permute-start.2 = (bf16[1024,128]{1,0:T(8,128)(2,1)}, bf16[1024,128]{1,0:T(8,128)(2,1)S(1)}, u32[]{:S(2)}, u32[]{:S(2)}) collective-permute-start(bf16[1024,128]{1,0:T(8,128)(2,1)} %rest_1_), channel_id=1, source_target_pairs={{0,128},{32,160},{64,192},{96,224},{128,0},{160,32},{192,64},{224,... | collective-permute-start | bytes 786440 | tf_op jit(solution)/shard_map/ppermute | solution.py:331
  6.2 1.1 collective-permute-start.3
  7.2 0.0 collective-permute-done.other_ref.rest_2_
  7.2 0.0 copy-start
  7.2 1.0 copy-done
  8.2 0.8 copy-done.2
  9.0 0.4 prepare.1
  9.4 4.4 %collective-permute-done.1.rest_3_ = bf16[1024,128]{1,0:T(8,128)(2,1)S(1)} collective-permute-done((bf16[1024,128]{1,0:T(8,128)(2,1)}, bf16[1024,128]{1,0:T(8,128)(2,1)S(1)}, u32[]{:S(2)}, u32[]{:S(2)}) %collective-permute-start.1) | collective-permute-done | bytes 262176 | tf_op jit(solution)/shard_map/ppermute | solution.py:331
  13.7 4.7 %collective-permute-done.2.rest_5_ = bf16[1024,128]{1,0:T(8,128)(2,1)S(1)} collective-permute-done((bf16[1024,128]{1,0:T(8,128)(2,1)}, bf16[1024,128]{1,0:T(8,128)(2,1)S(1)}, u32[]{:S(2)}, u32[]{:S(2)}) %collective-permute-start.2) | collective-permute-done | bytes 262176 | tf_op jit(solution)/shard_map/ppermute | solution.py:331
  18.4 0.8 collective-permute-done.3.rest_7_
  19.2 17.3 %collective-permute-start.4 = (bf16[1024,128]{1,0:T(8,128)(2,1)S(1)}, bf16[1024,128]{1,0:T(8,128)(2,1)S(1)}, u32[]{:S(2)}, u32[]{:S(2)}) collective-permute-start(bf16[1024,128]{1,0:T(8,128)(2,1)S(1)} %collective-permute-done.1.rest_3_), channel_id=1, source_target_pairs={{0,32},{32,0},{64,96},{96,64},{128,160},{160,128},{192,224},{224,1... | collective-permute-start | bytes 786440 | tf_op jit(solution)/shard_map/ppermute | solution.py:360
  36.5 0.1 collective-permute-start.5
  36.6 0.4 collective-permute-start.6
  37.7 0.7 fusion.items_ref
  38.3 0.0 collective-permute-done.4.rest_4_
  38.3 0.0 collective-permute-done.5.rest_6_
  38.4 0.0 collective-permute-done.6.rest_8_
  38.4 18.0 %conditional.3 = (bf16[32,80,128]{2,1,0:T(8,128)(2,1)S(1)}) conditional(s32[]{:T(128)} %convert_element_type.11, bf16[32,80,128]{2,1,0:T(8,128)(2,1)S(1)} %get-tuple-element.68, bf16[32,80,128]{2,1,0:T(8,128)(2,1)S(1)} %get-tuple-element.68), branch_computations={%region_2.3_spmd, %region_3.4_spmd} | conditional | bytes 2621448 | solution.py:362
  38.4 18.0 %all_to_all.44 = bf16[32,80,128]{2,1,0:T(8,128)(2,1)S(1)} all-to-all(bf16[32,80,128]{2,1,0:T(8,128)(2,1)S(1)} %copy.14), channel_id=1, replica_groups=mesh['row'=8,'col'=32] {'col'}, dimensions={0} | all-to-all | bytes 1310720 | tf_op jit(solution)/shard_map/cond/branch_0_fun/all_to_all | solution.py:325
  56.5 0.1 collective-permute-start.9
  56.6 2.2 %collective-permute-start.8 = (f32[4,128]{1,0:T(4,128)S(1)}, f32[4,128]{1,0:T(4,128)S(1)}, u32[]{:S(2)}, u32[]{:S(2)}) collective-permute-start(f32[4,128]{1,0:T(4,128)S(1)} %slice_add_fusion), channel_id=1, source_target_pairs={{0,128},{32,160},{64,192},{96,224},{128,0},{160,32},{192,64},{224,... | collective-permute-start | bytes 6152 | tf_op jit(solution)/shard_map/ppermute | solution.py:331
  58.7 0.0 collective-permute-start.7
  58.7 0.0 copy-done.4
  58.7 0.0 copy-done.1
  58.7 0.0 copy-start.3
  58.8 7.7 %tile_start.1 = (s16[32,80,128]{2,1,0:T(8,128)(2,1)S(1)}, bf16[8192,128]{1,0:T(8,128)(2,1)S(1)}, bf16[40,256,256]{2,1,0:T(8,128)(2,1)S(1)}) custom-call(s32[40]{0:T(128)S(1)} %bitcast.17, s32[40]{0:T(128)S(1)} %fusion.items_ref, s32[40,256,256]{2,1,0:T(8,128)} %bitcast.21, bf16[32,80,128]{2,1,0:T(8,128)(2,1)S(1)} %get-tuple-element.69.rows_ref, ...), custom_call_target="tpu_custom_call" | custom-call | flops 1342177280 | bytes 10485760 | tf_op jit(solution)/shard_map/tile_start/pallas_call | solution.py:149
  66.5 0.0 collective-permute-done.9
  66.5 0.0 collective-permute-done.8
  66.5 0.0 collective-permute-done.7
  66.5 0.1 insert.1
  66.6 20.8 %all_to_all.45.parts_ref = s16[32,80,128]{2,1,0:T(8,128)(2,1)S(1)} all-to-all(s16[32,80,128]{2,1,0:T(8,128)(2,1)S(1)} %insert.1), channel_id=1, replica_groups=mesh['row'=8,'col'=32] {'col'}, dimensions={0} | all-to-all | bytes 1310720 | tf_op jit(solution)/shard_map/all_to_all | solution.py:325
  87.4 0.0 copy-done.3
  87.4 0.4 start_update.1
  87.7 19.0 %all_to_all.46.rows_ref = bf16[32,64,128]{2,1,0:T(8,128)(2,1)S(1)} all-to-all(bf16[32,64,128]{2,1,0:T(8,128)(2,1)S(1)} %get-tuple-element.56), channel_id=1, replica_groups=mesh['row'=8,'col'=32] {'col'}, dimensions={0} | all-to-all | bytes 1048576 | tf_op jit(solution)/shard_map/all_to_all | solution.py:325
  106.8 3.9 %tile_pass.3 = s16[32,72,128]{2,1,0:T(8,128)(2,1)S(1)} custom-call(s32[40]{0:T(128)S(1)} %bitcast.18, s32[40]{0:T(128)S(1)} %fusion.items_ref, bf16[40,256,256]{2,1,0:T(8,128)(2,1)S(1)} %get-tuple-element.54.rates, bf16[32,64,128]{2,1,0:T(8,128)(2,1)S(1)} %all_to_all.46.rows_ref, bf16[8192,128]{1,0:T(8,128)(2,1)S(1)} %get-tuple-element.57.rest_0_), custom_call_target="tpu_custom_call" | custom-call | flops 1342177280 | bytes 5242880 | tf_op jit(solution)/shard_map/tile_pass/pallas_call | solution.py:149
  110.7 18.4 %all_to_all.47.parts_ref = s16[32,72,128]{2,1,0:T(8,128)(2,1)S(1)} all-to-all(s16[32,72,128]{2,1,0:T(8,128)(2,1)S(1)} %tile_pass.3), channel_id=1, replica_groups=mesh['row'=8,'col'=32] {'col'}, dimensions={0} | all-to-all | bytes 1179648 | tf_op jit(solution)/shard_map/all_to_all | solution.py:325
  129.2 0.5 update.2
  129.6 18.4 %all_to_all.48.rows_ref = bf16[32,64,128]{2,1,0:T(8,128)(2,1)S(1)} all-to-all(bf16[32,64,128]{2,1,0:T(8,128)(2,1)S(1)} %get-tuple-element.60), channel_id=1, replica_groups=mesh['row'=8,'col'=32] {'col'}, dimensions={0} | all-to-all | bytes 1048576 | tf_op jit(solution)/shard_map/all_to_all | solution.py:325
  148.1 3.9 %tile_pass.4 = s16[32,72,128]{2,1,0:T(8,128)(2,1)S(1)} custom-call(s32[40]{0:T(128)S(1)} %bitcast.19, s32[40]{0:T(128)S(1)} %fusion.items_ref, bf16[40,256,256]{2,1,0:T(8,128)(2,1)S(1)} %get-tuple-element.54.rates, bf16[32,64,128]{2,1,0:T(8,128)(2,1)S(1)} %all_to_all.48.rows_ref, bf16[8192,128]{1,0:T(8,128)(2,1)S(1)} %get-tuple-element.57.rest_0_), custom_call_target="tpu_custom_call" | custom-call | flops 1342177280 | bytes 5242880 | tf_op jit(solution)/shard_map/tile_pass/pallas_call | solution.py:149
  152.0 17.2 %all_to_all.49.parts_ref = s16[32,72,128]{2,1,0:T(8,128)(2,1)S(1)} all-to-all(s16[32,72,128]{2,1,0:T(8,128)(2,1)S(1)} %tile_pass.4), channel_id=1, replica_groups=mesh['row'=8,'col'=32] {'col'}, dimensions={0} | all-to-all | bytes 1179648 | tf_op jit(solution)/shard_map/all_to_all | solution.py:325
  169.2 0.5 update.3
  169.7 16.8 %all_to_all.50.rows_ref = bf16[32,64,128]{2,1,0:T(8,128)(2,1)S(1)} all-to-all(bf16[32,64,128]{2,1,0:T(8,128)(2,1)S(1)} %get-tuple-element.64), channel_id=1, replica_groups=mesh['row'=8,'col'=32] {'col'}, dimensions={0} | all-to-all | bytes 1048576 | tf_op jit(solution)/shard_map/all_to_all | solution.py:325
  186.5 3.9 %tile_pass.5 = s16[32,72,128]{2,1,0:T(8,128)(2,1)S(1)} custom-call(s32[40]{0:T(128)S(1)} %bitcast.20, s32[40]{0:T(128)S(1)} %fusion.items_ref, bf16[40,256,256]{2,1,0:T(8,128)(2,1)S(1)} %get-tuple-element.54.rates, bf16[32,64,128]{2,1,0:T(8,128)(2,1)S(1)} %all_to_all.50.rows_ref, bf16[8192,128]{1,0:T(8,128)(2,1)S(1)} %get-tuple-element.57.rest_0_), custom_call_target="tpu_custom_call" | custom-call | flops 1342177280 | bytes 5242880 | tf_op jit(solution)/shard_map/tile_pass/pallas_call | solution.py:149
  190.5 17.1 %all_to_all.51.parts_ref = s16[32,72,128]{2,1,0:T(8,128)(2,1)S(1)} all-to-all(s16[32,72,128]{2,1,0:T(8,128)(2,1)S(1)} %tile_pass.5), channel_id=1, replica_groups=mesh['row'=8,'col'=32] {'col'}, dimensions={0} | all-to-all | bytes 1179648 | tf_op jit(solution)/shard_map/all_to_all | solution.py:325
  207.6 1.0 update_last.1
  (7 shorter events, 0.1 us)
Async XLA Ops:
  0.6 58.1 %copy-start.4 = (s32[1,1,40]{2,1,0:T(1,128)S(1)}, s32[1,1,40]{2,1,0:T(1,128)}, u32[]{:S(2)}) copy-start(s32[1,1,40]{2,1,0:T(1,128)} %param.12) | copy-start | bytes 484
  0.6 6.6 %collective-permute-start = (bf16[1024,128]{1,0:T(8,128)(2,1)}, bf16[1024,128]{1,0:T(8,128)(2,1)S(1)}, u32[]{:S(2)}, u32[]{:S(2)}) collective-permute-start(bf16[1024,128]{1,0:T(8,128)(2,1)} %rest_1_), channel_id=1, source_target_pairs={{0,32},{32,0},{64,96},{96,64},{128,160},{160,128},{192,224},{224,1... | collective-permute-start | bytes 786440 | tf_op jit(solution)/shard_map/ppermute | solution.py:351
  4.0 9.8 %collective-permute-start.1 = (bf16[1024,128]{1,0:T(8,128)(2,1)}, bf16[1024,128]{1,0:T(8,128)(2,1)S(1)}, u32[]{:S(2)}, u32[]{:S(2)}) collective-permute-start(bf16[1024,128]{1,0:T(8,128)(2,1)} %rest_1_), channel_id=1, source_target_pairs={{0,64},{32,96},{64,128},{96,160},{128,192},{160,224},{192,0},{224,... | collective-permute-start | bytes 786440 | tf_op jit(solution)/shard_map/ppermute | solution.py:331
  4.0 14.5 %collective-permute-start.2 = (bf16[1024,128]{1,0:T(8,128)(2,1)}, bf16[1024,128]{1,0:T(8,128)(2,1)S(1)}, u32[]{:S(2)}, u32[]{:S(2)}) collective-permute-start(bf16[1024,128]{1,0:T(8,128)(2,1)} %rest_1_), channel_id=1, source_target_pairs={{0,128},{32,160},{64,192},{96,224},{128,0},{160,32},{192,64},{224,... | collective-permute-start | bytes 786440 | tf_op jit(solution)/shard_map/ppermute | solution.py:331
  6.2 13.0 %collective-permute-start.3 = (bf16[1024,128]{1,0:T(8,128)(2,1)}, bf16[1024,128]{1,0:T(8,128)(2,1)S(1)}, u32[]{:S(2)}, u32[]{:S(2)}) collective-permute-start(bf16[1024,128]{1,0:T(8,128)(2,1)} %rest_1_), channel_id=1, source_target_pairs={{0,192},{32,224},{64,0},{96,32},{128,64},{160,96},{192,128},{224,1... | collective-permute-start | bytes 786440 | tf_op jit(solution)/shard_map/ppermute | solution.py:331
  7.2 1.0 copy-start
  8.2 0.8 copy-start.2
  9.0 49.8 %copy-start.1 = (bf16[1024,128]{1,0:T(8,128)(2,1)S(1)}, bf16[1024,128]{1,0:T(8,128)(2,1)}, u32[]{:S(2)}) copy-start(bf16[1024,128]{1,0:T(8,128)(2,1)} %rest_1_) | copy-start | bytes 786436
  19.2 19.2 %collective-permute-start.4 = (bf16[1024,128]{1,0:T(8,128)(2,1)S(1)}, bf16[1024,128]{1,0:T(8,128)(2,1)S(1)}, u32[]{:S(2)}, u32[]{:S(2)}) collective-permute-start(bf16[1024,128]{1,0:T(8,128)(2,1)S(1)} %collective-permute-done.1.rest_3_), channel_id=1, source_target_pairs={{0,32},{32,0},{64,96},{96,64},{128,160},{160,128},{192,224},{224,1... | collective-permute-start | bytes 786440 | tf_op jit(solution)/shard_map/ppermute | solution.py:360
  36.5 1.9 collective-permute-start.5
  36.6 1.8 collective-permute-start.6
  56.5 10.0 %collective-permute-start.9 = (f32[4,128]{1,0:T(4,128)S(1)}, f32[4,128]{1,0:T(4,128)S(1)}, u32[]{:S(2)}, u32[]{:S(2)}) collective-permute-start(f32[4,128]{1,0:T(4,128)S(1)} %slice_add_fusion), channel_id=1, source_target_pairs={{0,192},{32,224},{64,0},{96,32},{128,64},{160,96},{192,128},{224,1... | collective-permute-start | bytes 6152 | tf_op jit(solution)/shard_map/ppermute | solution.py:331
  56.6 9.9 %collective-permute-start.8 = (f32[4,128]{1,0:T(4,128)S(1)}, f32[4,128]{1,0:T(4,128)S(1)}, u32[]{:S(2)}, u32[]{:S(2)}) collective-permute-start(f32[4,128]{1,0:T(4,128)S(1)} %slice_add_fusion), channel_id=1, source_target_pairs={{0,128},{32,160},{64,192},{96,224},{128,0},{160,32},{192,64},{224,... | collective-permute-start | bytes 6152 | tf_op jit(solution)/shard_map/ppermute | solution.py:331
  58.7 7.8 %collective-permute-start.7 = (f32[4,128]{1,0:T(4,128)S(1)}, f32[4,128]{1,0:T(4,128)S(1)}, u32[]{:S(2)}, u32[]{:S(2)}) collective-permute-start(f32[4,128]{1,0:T(4,128)S(1)} %slice_add_fusion), channel_id=1, source_target_pairs={{0,64},{32,96},{64,128},{96,160},{128,192},{160,224},{192,0},{224,... | collective-permute-start | bytes 6152 | tf_op jit(solution)/shard_map/ppermute | solution.py:331
  58.7 28.6 %copy-start.3 = (f32[64,128]{1,0:T(8,128)S(1)}, f32[64,128]{1,0:T(8,128)}, u32[]{:S(2)}) copy-start(f32[64,128]{1,0:T(8,128)} %factors_ref.1) | copy-start | bytes 98308
